TPU v7x, 256 devices: a whole 4x4x8 slice. The times are simulated.
256 devices in a mesh: src: 32 (over z, y_lo, core), slab: 8 (over x, y_hi).
Axes of the slice: x: 4, y: 4 (y_hi: 2, y_lo: 2; y = y_hi * 2 + y_lo), z: 8, core: 2. Of those that a mesh axis runs over, the one named last changes fastest.
Arguments:
- forward_field: float32 [32, 32, 384, 384], P('src', 'slab'), may hold values from -6 to 6
- misfit: float32 [32, 9216], P('src', 'slab'), may hold values from -6 to 6
- receivers: int32 [32, 9216, 2], P('src', 'slab'), may hold values from 0 to 147455, as said below
- classes: int32 [32, 384, 384], P('slab'), may hold values from 0 to 15
- table: float32 [16], replicated, may hold values from 0.3 to 3
Outputs:
- adjoint_field: float32 [32, 32, 384, 384], P('src', 'slab')
- gradient: float32 [32, 384, 384], P('slab', 'src')
Inputs may be any that keep to these rules, and one draw needn't show every extreme that they name: `receivers`: entries of block k of 1152 entries along the second dimension have a first coordinate z with k * 4 <= z < (k + 1) * 4, and an index within the layer from 0 to 147455; the same cell may appear several times.
All inputs are finite; a program needn't handle non-finite values.
Results may differ from a plain program's by a relative error of at most 0.0003.
Values sent between devices are 32-bit elements; how exact they have to be, the bound alone decides.
No kernel may reach another device: no remote copies, remote signals or barrier semaphores. Data moves between devices by JAX's collectives and lax.ppermute only.
A program may use at most 128 MiB of HBM per device.

v0:
```python
import jax
import jax.numpy as jnp
from jax import lax
from jax.sharding import PartitionSpec as P

ITERS = 3


def with_halo(cells, sides, width):
    for axis, dim in sides:
        count = lax.axis_size(axis)
        ends = count - 1
        head = lax.slice_in_dim(cells, 0, width, axis=dim)
        tail = lax.slice_in_dim(cells, cells.shape[dim] - width, cells.shape[dim], axis=dim)
        cells = jnp.concatenate(
            [
                lax.ppermute(tail, axis, [(i, (i + 1) % count) for i in range(ends)]),
                cells,
                lax.ppermute(head, axis, [((i + 1) % count, i) for i in range(ends)]),
            ],
            axis=dim,
        )
    return cells


def neighbours(padded):
    inner = padded[..., 1:-1, :, :]
    spread = [(0, 0)] * (padded.ndim - 2) + [(1, 1), (1, 1)]
    side = jnp.pad(inner, spread)
    return (
        inner,
        [
            padded[..., 2:, :, :],
            padded[..., :-2, :, :],
            side[..., 2:, 1:-1],
            side[..., :-2, 1:-1],
            side[..., 1:-1, 2:],
            side[..., 1:-1, :-2],
        ],
    )


def operate(field, couplings, diagonal):
    padded = with_halo(field, (("slab", 1),), 1)
    inner, besides = neighbours(padded)
    result = diagonal * field
    for coupling, beside in zip(couplings, besides):
        result = result - coupling * beside
    return result


def cells_sum(first, second):
    return jnp.sum(first * second, axis=(1, 2, 3))


def norm_sum(residual, precond):
    return lax.psum(cells_sum(residual, precond), "slab")


def expand(values):
    return values[:, None, None, None]


def body(forward_field, misfit, receivers, classes, table):
    sources_here, layers, rows_y, columns = forward_field.shape
    cells = layers * rows_y * columns
    labels = jnp.arange(table.shape[0], dtype=jnp.int32)
    conduct = jnp.sum(
        jnp.where(classes[None] == labels[:, None, None, None], table[:, None, None, None], 0.0),
        axis=0,
    )
    stacked = jnp.concatenate([conduct[None], forward_field], axis=0)
    planes = with_halo(stacked, (("slab", 1),), 1)
    conduct_pad = planes[0]
    forward_pad = planes[1:]
    conduct_in, conduct_near = neighbours(conduct_pad)
    couplings = [0.5 * (conduct + beside) for beside in conduct_near]
    diagonal = couplings[0]
    for coupling in couplings[1:]:
        diagonal = diagonal + coupling
    local = (receivers[..., 0] - lax.axis_index("slab") * layers) * (rows_y * columns) + receivers[
        ..., 1
    ]
    offsets = jnp.arange(sources_here, dtype=jnp.int32)[:, None] * cells
    right_side = (
        jnp.zeros((sources_here * cells,), jnp.float32)
        .at[(local + offsets).reshape(-1)]
        .add(misfit.reshape(-1))
    )
    right_side = right_side.reshape(sources_here, layers, rows_y, columns)
    adjoint = jnp.zeros_like(right_side)
    residual = right_side
    precond = residual / diagonal
    direction = precond
    inner_rz = norm_sum(residual, precond)
    for number in range(ITERS):
        image = operate(direction, couplings, diagonal)
        curve = lax.psum(cells_sum(direction, image), "slab")
        step_size = expand(inner_rz / curve)
        adjoint = adjoint + step_size * direction
        residual = residual - step_size * image
        precond = residual / diagonal
        inner_new = norm_sum(residual, precond)
        direction = precond + expand(inner_new / inner_rz) * direction
        inner_rz = inner_new
    adjoint_pad = with_halo(adjoint, (("slab", 1),), 1)
    forward_in, forward_near = neighbours(forward_pad)
    adjoint_in, adjoint_near = neighbours(adjoint_pad)
    term = jnp.zeros((layers, rows_y, columns), jnp.float32)
    for forward_side, adjoint_side in zip(forward_near, adjoint_near):
        term = term + jnp.sum((forward_in - forward_side) * (adjoint_in - adjoint_side), axis=0)
    term = -0.5 * term
    gradient = lax.psum_scatter(term, "src", scatter_dimension=1, tiled=True)
    return (adjoint, gradient)


def solution(mesh):
    placed = (
        P("src", "slab", None, None),
        P("src", "slab"),
        P("src", "slab", None),
        P("slab", None, None),
        P(),
    )
    return jax.shard_map(
        body,
        mesh=mesh,
        in_specs=placed,
        out_specs=(P("src", "slab", None, None), P("slab", "src", None)),
        check_vma=False,
    )
```

profile of v0, /device:TPU:1, one launch (start us, length us, event | category | flops | bytes accessed | tf_op | source)
XLA Modules:
  0.0 603.0 jit_solution(17939996561863353005)
XLA Ops:
  7.2 0.0 all-reduce.10.cloned.1.call-start
  7.2 0.0 copy-start.4
  7.2 5.8 select_reduce_fusion
  13.1 0.0 copy-done.4
  13.1 0.0 copy-start.13
  13.1 1.5 pad_maximum_fusion.15
  14.6 1.3 collective-permute-start
  15.9 7.3 %collective-permute-start.1 = (f32[2,1,384,384]{3,2,1,0:T(8,128)}, f32[2,1,384,384]{3,2,1,0:T(8,128)}, u32[]{:S(2)}, u32[]{:S(2)}) collective-permute-start(f32[2,1,384,384]{3,2,1,0:T(8,128)} %get-tuple-element.20), channel_id=1, source_target_pairs={{0,1},{1,2},{2,3},{3,4},{4,5},{5,6},{6,7},{8,9},{9,10},{10,11},{11... | collective-permute-start | bytes 3538952 | tf_op jit(solution)/shard_map/ppermute | solution.py:17
  23.2 1.3 reduce.8
  24.5 0.6 fusion.80
  25.2 9.0 %scatter_custom_fusion = f32[589824]{0:T(1024)} fusion(s32[1152]{0:T(1024)} %fusion.80, f32[1152]{0:T(1024)} %reduce.8, f32[]{:T(128)} %constant.8.clone.1), kind=kCustom, calls=%fused_computation.139 | custom fusion | flops 1152 | bytes 2359808 | tf_op jit(solution)/shard_map/scatter-add | solution.py:88
  34.1 3.4 reshape.106
  37.5 6.5 %collective-permute-done = f32[2,1,384,384]{3,2,1,0:T(8,128)S(1)} collective-permute-done((f32[2,1,384,384]{3,2,1,0:T(8,128)}, f32[2,1,384,384]{3,2,1,0:T(8,128)S(1)}, u32[]{:S(2)}, u32[]{:S(2)}) %collective-permute-start) | collective-permute-done | bytes 1179680 | tf_op jit(solution)/shard_map/ppermute | solution.py:19
  44.0 28.4 %collective-permute-done.1 = f32[2,1,384,384]{3,2,1,0:T(8,128)} collective-permute-done((f32[2,1,384,384]{3,2,1,0:T(8,128)}, f32[2,1,384,384]{3,2,1,0:T(8,128)}, u32[]{:S(2)}, u32[]{:S(2)}) %collective-permute-start.1) | collective-permute-done | bytes 1179680 | tf_op jit(solution)/shard_map/ppermute | solution.py:17
  72.4 5.4 multiply_reduce_fusion.4
  77.8 1.4 copy-done.2
  79.2 1.1 fusion.87
  80.4 1.3 collective-permute-start.2
  81.6 7.1 %collective-permute-start.3 = (f32[1,1,384,384]{3,2,1,0:T(8,128)}, f32[1,1,384,384]{3,2,1,0:T(8,128)}, u32[]{:S(2)}, u32[]{:S(2)}) collective-permute-start(f32[1,1,384,384]{3,2,1,0:T(8,128)} %get-tuple-element.28), channel_id=1, source_target_pairs={{0,1},{1,2},{2,3},{3,4},{4,5},{5,6},{6,7},{8,9},{9,10},{10,11},{11... | collective-permute-start | bytes 1769480 | tf_op jit(solution)/shard_map/ppermute | solution.py:17
  88.7 3.4 reshape.107
  92.1 7.4 %collective-permute-done.2 = f32[1,1,384,384]{3,2,1,0:T(8,128)} collective-permute-done((f32[1,1,384,384]{3,2,1,0:T(8,128)}, f32[1,1,384,384]{3,2,1,0:T(8,128)}, u32[]{:S(2)}, u32[]{:S(2)}) %collective-permute-start.2) | collective-permute-done | bytes 589856 | tf_op jit(solution)/shard_map/ppermute | solution.py:19
  99.5 13.3 %collective-permute-done.3 = f32[1,1,384,384]{3,2,1,0:T(8,128)} collective-permute-done((f32[1,1,384,384]{3,2,1,0:T(8,128)}, f32[1,1,384,384]{3,2,1,0:T(8,128)}, u32[]{:S(2)}, u32[]{:S(2)}) %collective-permute-start.3) | collective-permute-done | bytes 589856 | tf_op jit(solution)/shard_map/ppermute | solution.py:17
  112.9 0.0 copy-done.11
  112.9 12.6 %multiply_reduce_fusion.3 = (f32[]{:T(128)}, f32[1,4,384,384]{3,2,1,0:T(8,128)}, f32[1,4,384,384]{3,2,1,0:T(8,128)}, f32[1,4,384,384]{3,2,1,0:T(8,128)}) fusion(f32[4,384,384]{2,1,0:T(8,128)} %copy-done.2, f32[4,384,384]{2,1,0:T(8,128)S(1)} %select_reduce_fusion, f32[1,4,384,384]{3,2,1,0:T(8,128)} %bitcast.97, ...), kind=kLoop, calls=%fused_computation.133 | loop fusion | flops 19464192 | bytes 24772612 | tf_op jit(solution)/shard_map/reduce_sum | solution.py:53
  125.4 20.5 %all-reduce.7 = (f32[1]{0:T(128)}, f32[1]{0:T(128)}) all-reduce(f32[1]{0:T(128)} %bitcast.4, f32[1]{0:T(128)} %bitcast.11), channel_id=1, replica_groups=mesh['src'=32,'slab'=8] {'slab'}, use_global_device_ids=true, to_apply=%region_3.4 | all-reduce | flops 2 | bytes 16 | tf_op jit(solution)/shard_map/psum | solution.py:57
  147.2 5.7 multiply_reduce_fusion.2
  152.9 16.1 %psum.44 = f32[1]{0:T(128)} all-reduce(f32[1]{0:T(128)} %bitcast.15), channel_id=1, replica_groups=mesh['src'=32,'slab'=8] {'slab'}, use_global_device_ids=true, to_apply=%region_7.8 | all-reduce | flops 1 | bytes 8 | tf_op jit(solution)/shard_map/psum | solution.py:57
  170.4 0.0 copy-start.6
  170.4 3.6 bitcast_add_fusion
  173.9 0.1 fusion.86
  174.0 1.7 collective-permute-start.4
  175.8 6.4 %collective-permute-start.5 = (f32[1,1,384,384]{3,2,1,0:T(8,128)S(1)}, f32[1,1,384,384]{3,2,1,0:T(8,128)}, u32[]{:S(2)}, u32[]{:S(2)}) collective-permute-start(f32[1,1,384,384]{3,2,1,0:T(8,128)S(1)} %get-tuple-element.26), channel_id=1, source_target_pairs={{0,1},{1,2},{2,3},{3,4},{4,5},{5,6},{6,7},{8,9},{9,10},{10,11},{11... | collective-permute-start | bytes 1769480 | tf_op jit(solution)/shard_map/ppermute | solution.py:17
  182.1 4.6 collective-permute-done.4
  186.8 17.4 %collective-permute-done.5 = f32[1,1,384,384]{3,2,1,0:T(8,128)} collective-permute-done((f32[1,1,384,384]{3,2,1,0:T(8,128)S(1)}, f32[1,1,384,384]{3,2,1,0:T(8,128)}, u32[]{:S(2)}, u32[]{:S(2)}) %collective-permute-start.5) | collective-permute-done | bytes 589856 | tf_op jit(solution)/shard_map/ppermute | solution.py:17
  204.2 6.8 %multiply_reduce_fusion.1 = (f32[]{:T(128)}, f32[1,4,384,384]{3,2,1,0:T(8,128)}) fusion(f32[1,4,384,384]{3,2,1,0:T(8,128)S(1)} %bitcast_add_fusion, f32[4,384,384]{2,1,0:T(8,128)S(1)} %select_reduce_fusion, f32[1,4,384,384]{3,2,1,0:T(8,128)} %get-tuple-element.15, f32[1,1,384,384]{3,2,1,0:T(8,128)} %collective-permute-done.5, ...), kind=kLoop, calls=%fused_computation.130 | loop fusion | flops 14745599 | bytes 15335428 | tf_op jit(solution)/shard_map/reduce_sum | solution.py:53
  211.0 0.0 copy-done.3
  211.0 19.9 %psum.45 = f32[1]{0:T(128)} all-reduce(f32[1]{0:T(128)} %bitcast.18), channel_id=1, replica_groups=mesh['src'=32,'slab'=8] {'slab'}, use_global_device_ids=true, to_apply=%region_9.10 | all-reduce | flops 1 | bytes 8 | tf_op jit(solution)/shard_map/psum | solution.py:98
  232.2 4.3 multiply_reduce_fusion
  236.6 16.1 %psum.46 = f32[1]{0:T(128)} all-reduce(f32[1]{0:T(128)} %bitcast.20), channel_id=1, replica_groups=mesh['src'=32,'slab'=8] {'slab'}, use_global_device_ids=true, to_apply=%region_11.12 | all-reduce | flops 1 | bytes 8 | tf_op jit(solution)/shard_map/psum | solution.py:57
  253.9 4.4 multiply_add_fusion
  258.3 0.0 copy-start.9
  258.3 1.4 copy-done.9
  259.7 0.1 fusion.85
  259.7 1.4 collective-permute-start.6
  261.2 5.5 collective-permute-start.7
  266.7 5.3 collective-permute-done.6
  272.0 15.3 %collective-permute-done.7 = f32[1,1,384,384]{3,2,1,0:T(8,128)S(1)} collective-permute-done((f32[1,1,384,384]{3,2,1,0:T(8,128)S(1)}, f32[1,1,384,384]{3,2,1,0:T(8,128)S(1)}, u32[]{:S(2)}, u32[]{:S(2)}) %collective-permute-start.7) | collective-permute-done | bytes 589856 | tf_op jit(solution)/shard_map/ppermute | solution.py:17
  287.3 8.7 %fusion.30 = f32[]{:T(128)} fusion(f32[1,4,384,384]{3,2,1,0:T(8,128)} %copy-done.9, f32[1,4,384,384]{3,2,1,0:T(8,128)S(1)} %copy-done.8, f32[1,1,384,384]{3,2,1,0:T(8,128)S(1)} %collective-permute-done.7, f32[1,4,384,384]{3,2,1,0:T(8,128)S(1)} %copy-done.7, f32[1,1,384,384]{3,2,1,0:T(8,128)S(1)} %collective-permute-done.6, f32[4,384,384]{2,1,0:T(8,128)S(1)} %copy-done.1, ...), kind=kLoop, calls=%fused_computation.57 | loop fusion | flops 14745599 | bytes 12976132 | tf_op jit(solution)/shard_map/reduce_sum | solution.py:53
  296.0 19.8 %psum.47 = f32[1]{0:T(128)} all-reduce(f32[1]{0:T(128)} %bitcast.22), channel_id=1, replica_groups=mesh['src'=32,'slab'=8] {'slab'}, use_global_device_ids=true, to_apply=%region_13.14 | all-reduce | flops 1 | bytes 8 | tf_op jit(solution)/shard_map/psum | solution.py:98
  317.1 5.4 fusion.71
  322.4 0.0 copy-start.10
  322.5 0.0 copy-start.5
  322.5 0.1 fusion.84
  322.6 1.6 collective-permute-start.8
  324.1 6.3 %collective-permute-start.9 = (f32[1,1,384,384]{3,2,1,0:T(8,128)S(1)}, f32[1,1,384,384]{3,2,1,0:T(8,128)}, u32[]{:S(2)}, u32[]{:S(2)}) collective-permute-start(f32[1,1,384,384]{3,2,1,0:T(8,128)S(1)} %get-tuple-element.22), channel_id=1, source_target_pairs={{0,1},{1,2},{2,3},{3,4},{4,5},{5,6},{6,7},{8,9},{9,10},{10,11},{11... | collective-permute-start | bytes 1769480 | tf_op jit(solution)/shard_map/ppermute | solution.py:17
  330.4 4.6 collective-permute-done.8
  335.1 13.0 %collective-permute-done.9 = f32[1,1,384,384]{3,2,1,0:T(8,128)} collective-permute-done((f32[1,1,384,384]{3,2,1,0:T(8,128)S(1)}, f32[1,1,384,384]{3,2,1,0:T(8,128)}, u32[]{:S(2)}, u32[]{:S(2)}) %collective-permute-start.9) | collective-permute-done | bytes 589856 | tf_op jit(solution)/shard_map/ppermute | solution.py:17
  348.1 6.1 %fusion.41 = f32[4,384,384]{2,1,0:T(8,128)} fusion(f32[1,4,384,384]{3,2,1,0:T(8,128)S(1)} %copy-done.5, f32[1,4,384,384]{3,2,1,0:T(8,128)S(1)} %fusion.71, f32[1,1,384,384]{3,2,1,0:T(8,128)} %collective-permute-done.9, f32[2,1,384,384]{3,2,1,0:T(8,128)} %collective-permute-done.1, f32[1,4,384,384]{3,2,1,0:T(8,128)S(1)} %bitcast.95, ...), kind=kLoop, calls=%fused_computation.68 | loop fusion | flops 17694720 | bytes 12976128 | tf_op jit(solution)/shard_map/mul | solution.py:112
  354.2 4.6 copy.18
  358.8 0.0 all-reduce.10.cloned.1.call-update
  358.8 0.6 copy-done.14
  359.4 0.6 dynamic-slice
  360.7 233.9 %all-reduce.10.cloned.1.call-done = f32[4,384,384]{2,0,1:T(4,128)} async-done(((f32[4,384,384]{2,0,1:T(4,128)}), f32[4,384,384]{2,0,1:T(4,128)}) %all-reduce.10.cloned.1.call-update) | async-done | bytes 2359312
  594.6 1.5 constant_dynamic-slice_fusion
  (18 shorter events, 0.0 us)
Async XLA Ops:
  7.2 587.4 %all-reduce.10.cloned.1.call-start = ((), (), s32[]{:S(2)}) async-start(), calls=%async_computation | async-start | bytes 4718592
  7.2 5.9 copy-start.4
  13.1 11.5 %copy-start.13 = (s32[1,1152,2]{1,2,0:T(2,128)S(1)}, s32[1,1152,2]{1,2,0:T(2,128)}, u32[]{:S(2)}) copy-start(s32[1,1152,2]{1,2,0:T(2,128)} %param.7) | copy-start | bytes 27652
  14.6 29.4 %collective-permute-start = (f32[2,1,384,384]{3,2,1,0:T(8,128)}, f32[2,1,384,384]{3,2,1,0:T(8,128)S(1)}, u32[]{:S(2)}, u32[]{:S(2)}) collective-permute-start(f32[2,1,384,384]{3,2,1,0:T(8,128)} %get-tuple-element.19), channel_id=1, source_target_pairs={{1,0},{2,1},{3,2},{4,3},{5,4},{6,5},{7,6},{9,8},{10,9},{11,10},{12... | collective-permute-start | bytes 3538952 | tf_op jit(solution)/shard_map/ppermute | solution.py:19
  15.9 56.5 %collective-permute-start.1 = (f32[2,1,384,384]{3,2,1,0:T(8,128)}, f32[2,1,384,384]{3,2,1,0:T(8,128)}, u32[]{:S(2)}, u32[]{:S(2)}) collective-permute-start(f32[2,1,384,384]{3,2,1,0:T(8,128)} %get-tuple-element.20), channel_id=1, source_target_pairs={{0,1},{1,2},{2,3},{3,4},{4,5},{5,6},{6,7},{8,9},{9,10},{10,11},{11... | collective-permute-start | bytes 3538952 | tf_op jit(solution)/shard_map/ppermute | solution.py:17
  44.0 68.8 %copy-start.11 = (f32[2,1,384,384]{3,2,1,0:T(8,128)}, f32[2,1,384,384]{3,2,1,0:T(8,128)S(1)}, u32[]{:S(2)}) copy-start(f32[2,1,384,384]{3,2,1,0:T(8,128)S(1)} %collective-permute-done) | copy-start | bytes 3538948
  77.8 1.4 copy-start.2
  80.4 19.2 %collective-permute-start.2 = (f32[1,1,384,384]{3,2,1,0:T(8,128)}, f32[1,1,384,384]{3,2,1,0:T(8,128)}, u32[]{:S(2)}, u32[]{:S(2)}) collective-permute-start(f32[1,1,384,384]{3,2,1,0:T(8,128)} %get-tuple-element.27), channel_id=1, source_target_pairs={{1,0},{2,1},{3,2},{4,3},{5,4},{6,5},{7,6},{9,8},{10,9},{11,10},{12... | collective-permute-start | bytes 1769480 | tf_op jit(solution)/shard_map/ppermute | solution.py:19
  81.6 31.2 %collective-permute-start.3 = (f32[1,1,384,384]{3,2,1,0:T(8,128)}, f32[1,1,384,384]{3,2,1,0:T(8,128)}, u32[]{:S(2)}, u32[]{:S(2)}) collective-permute-start(f32[1,1,384,384]{3,2,1,0:T(8,128)} %get-tuple-element.28), channel_id=1, source_target_pairs={{0,1},{1,2},{2,3},{3,4},{4,5},{5,6},{6,7},{8,9},{9,10},{10,11},{11... | collective-permute-start | bytes 1769480 | tf_op jit(solution)/shard_map/ppermute | solution.py:17
  170.4 33.8 %copy-start.6 = (f32[1,4,384,384]{3,2,1,0:T(8,128)S(1)}, f32[1,4,384,384]{3,2,1,0:T(8,128)}, u32[]{:S(2)}) copy-start(f32[1,4,384,384]{3,2,1,0:T(8,128)} %get-tuple-element.14) | copy-start | bytes 7077892
  173.9 37.1 %copy-start.3 = (f32[1,4,384,384]{3,2,1,0:T(8,128)}, f32[1,4,384,384]{3,2,1,0:T(8,128)S(1)}, u32[]{:S(2)}) copy-start(f32[1,4,384,384]{3,2,1,0:T(8,128)S(1)} %bitcast_add_fusion) | copy-start | bytes 7077892
  173.9 30.2 %copy-start = (f32[4,384,384]{2,1,0:T(8,128)S(1)}, f32[4,384,384]{2,1,0:T(8,128)}, u32[]{:S(2)}) copy-start(f32[4,384,384]{2,1,0:T(8,128)} %get-tuple-element.18) | copy-start | bytes 7077892
  174.0 12.7 %collective-permute-start.4 = (f32[1,1,384,384]{3,2,1,0:T(8,128)S(1)}, f32[1,1,384,384]{3,2,1,0:T(8,128)}, u32[]{:S(2)}, u32[]{:S(2)}) collective-permute-start(f32[1,1,384,384]{3,2,1,0:T(8,128)S(1)} %get-tuple-element.25), channel_id=1, source_target_pairs={{1,0},{2,1},{3,2},{4,3},{5,4},{6,5},{7,6},{9,8},{10,9},{11,10},{12... | collective-permute-start | bytes 1769480 | tf_op jit(solution)/shard_map/ppermute | solution.py:19
  175.8 28.4 %collective-permute-start.5 = (f32[1,1,384,384]{3,2,1,0:T(8,128)S(1)}, f32[1,1,384,384]{3,2,1,0:T(8,128)}, u32[]{:S(2)}, u32[]{:S(2)}) collective-permute-start(f32[1,1,384,384]{3,2,1,0:T(8,128)S(1)} %get-tuple-element.26), channel_id=1, source_target_pairs={{0,1},{1,2},{2,3},{3,4},{4,5},{5,6},{6,7},{8,9},{9,10},{10,11},{11... | collective-permute-start | bytes 1769480 | tf_op jit(solution)/shard_map/ppermute | solution.py:17
  253.9 33.4 %copy-start.7 = (f32[1,4,384,384]{3,2,1,0:T(8,128)S(1)}, f32[1,4,384,384]{3,2,1,0:T(8,128)}, u32[]{:S(2)}) copy-start(f32[1,4,384,384]{3,2,1,0:T(8,128)} %get-tuple-element.14) | copy-start | bytes 7077892
  253.9 33.4 %copy-start.8 = (f32[1,4,384,384]{3,2,1,0:T(8,128)S(1)}, f32[1,4,384,384]{3,2,1,0:T(8,128)}, u32[]{:S(2)}) copy-start(f32[1,4,384,384]{3,2,1,0:T(8,128)} %get-tuple-element.15) | copy-start | bytes 7077892
  258.3 1.4 copy-start.9
  259.7 27.6 %copy-start.1 = (f32[4,384,384]{2,1,0:T(8,128)S(1)}, f32[4,384,384]{2,1,0:T(8,128)}, u32[]{:S(2)}) copy-start(f32[4,384,384]{2,1,0:T(8,128)} %get-tuple-element.18) | copy-start | bytes 7077892
  259.7 12.3 %collective-permute-start.6 = (f32[1,1,384,384]{3,2,1,0:T(8,128)S(1)}, f32[1,1,384,384]{3,2,1,0:T(8,128)S(1)}, u32[]{:S(2)}, u32[]{:S(2)}) collective-permute-start(f32[1,1,384,384]{3,2,1,0:T(8,128)S(1)} %get-tuple-element.23), channel_id=1, source_target_pairs={{1,0},{2,1},{3,2},{4,3},{5,4},{6,5},{7,6},{9,8},{10,9},{11,10},{12... | collective-permute-start | bytes 1769480 | tf_op jit(solution)/shard_map/ppermute | solution.py:19
  261.2 26.1 %collective-permute-start.7 = (f32[1,1,384,384]{3,2,1,0:T(8,128)S(1)}, f32[1,1,384,384]{3,2,1,0:T(8,128)S(1)}, u32[]{:S(2)}, u32[]{:S(2)}) collective-permute-start(f32[1,1,384,384]{3,2,1,0:T(8,128)S(1)} %get-tuple-element.24), channel_id=1, source_target_pairs={{0,1},{1,2},{2,3},{3,4},{4,5},{5,6},{6,7},{8,9},{9,10},{10,11},{11... | collective-permute-start | bytes 1769480 | tf_op jit(solution)/shard_map/ppermute | solution.py:17
  317.1 31.0 %copy-start.12 = (f32[2,1,384,384]{3,2,1,0:T(8,128)S(1)}, f32[2,1,384,384]{3,2,1,0:T(8,128)}, u32[]{:S(2)}) copy-start(f32[2,1,384,384]{3,2,1,0:T(8,128)} %copy-done.11) | copy-start | bytes 3538948
  322.4 31.7 %copy-start.10 = (f32[1,4,384,384]{3,2,1,0:T(8,128)}, f32[1,4,384,384]{3,2,1,0:T(8,128)S(1)}, u32[]{:S(2)}) copy-start(f32[1,4,384,384]{3,2,1,0:T(8,128)S(1)} %fusion.71) | copy-start | bytes 7077892
  322.5 25.6 %copy-start.5 = (f32[1,4,384,384]{3,2,1,0:T(8,128)S(1)}, f32[1,4,384,384]{3,2,1,0:T(8,128)}, u32[]{:S(2)}) copy-start(f32[1,4,384,384]{3,2,1,0:T(8,128)} %param.5) | copy-start | bytes 7077892
  322.6 12.5 %collective-permute-start.8 = (f32[1,1,384,384]{3,2,1,0:T(8,128)S(1)}, f32[1,1,384,384]{3,2,1,0:T(8,128)}, u32[]{:S(2)}, u32[]{:S(2)}) collective-permute-start(f32[1,1,384,384]{3,2,1,0:T(8,128)S(1)} %get-tuple-element.21), channel_id=1, source_target_pairs={{1,0},{2,1},{3,2},{4,3},{5,4},{6,5},{7,6},{9,8},{10,9},{11,10},{12... | collective-permute-start | bytes 1769480 | tf_op jit(solution)/shard_map/ppermute | solution.py:19
  324.1 23.9 %collective-permute-start.9 = (f32[1,1,384,384]{3,2,1,0:T(8,128)S(1)}, f32[1,1,384,384]{3,2,1,0:T(8,128)}, u32[]{:S(2)}, u32[]{:S(2)}) collective-permute-start(f32[1,1,384,384]{3,2,1,0:T(8,128)S(1)} %get-tuple-element.22), channel_id=1, source_target_pairs={{0,1},{1,2},{2,3},{3,4},{4,5},{5,6},{6,7},{8,9},{9,10},{10,11},{11... | collective-permute-start | bytes 1769480 | tf_op jit(solution)/shard_map/ppermute | solution.py:17
  358.7 0.7 copy-start.14
Sparse Core Ops, SparseCore 0:
  358.9 235.6 all-reduce.9
where the time goes:
time: 604 us; the launch traced here: 603 us
  waiting for transfers between devices  350 us (58%)
  blocking collectives  92.4 us (15%)
  other arithmetic  81.3 us (13%)
  starting transfers between devices  39.9 us (7%)
  between operations  21.2 us (4%)
  local copies, waits for them, and re-layouts  18.3 us (3%)
    unnamed x2, waiting for transfers between devices  234 us
    ppermute x5, waiting for transfers between devices, with_halo(): lax.ppermute(tail, axis, [(i, (i + 1) % count) for i in range(ends)])  87.4 us
    psum x3, blocking collectives, norm_sum(): return lax.psum(cells_sum(residual, precond), 'slab')  52.7 us
    reduce_sum x6, other arithmetic, cells_sum(): return jnp.sum(first * second, axis=(1, 2, 3))  43.6 us
    psum x2, blocking collectives, body(): curve = lax.psum(cells_sum(direction, image), 'slab')  39.7 us
    ppermute x5, starting transfers between devices, with_halo(): lax.ppermute(tail, axis, [(i, (i + 1) % count) for i in range(ends)])  32.6 us
    ppermute x5, waiting for transfers between devices, with_halo(): lax.ppermute(head, axis, [((i + 1) % count, i) for i in range(ends)])  28.5 us
  transfers between devices with their start and end apart: 11, of which 11 were waited for; matrix products, arithmetic and copies ran while one was open for 3% of the time, Pallas kernels for 0%

commit v1 on v0

v1 whole, which is shorter than its diff:
```python
import jax
import jax.numpy as jnp
from jax import lax
from jax.sharding import PartitionSpec as P

CORES = 2
Y_LO = 2


def lookup(classes, table):
    result = jnp.zeros(classes.shape, jnp.float32)
    for label in range(table.shape[0]):
        result = jnp.where(classes == label, table[label], result)
    return result


def slab_shift(value, step):
    count = lax.axis_size("slab")
    pairs = [(i, i + step) for i in range(count) if 0 <= i + step < count]
    return lax.ppermute(value, "slab", pairs)


def shifted(field, dim, step):
    spread = [(0, 0)] * field.ndim
    size = field.shape[dim]
    if step > 0:
        spread[dim] = (0, 1)
        return lax.slice_in_dim(jnp.pad(field, spread), 1, size + 1, axis=dim)
    spread[dim] = (1, 0)
    return lax.slice_in_dim(jnp.pad(field, spread), 0, size, axis=dim)


def near(field):
    inner = field[1:-1]
    return [
        field[2:],
        field[:-2],
        shifted(inner, 1, 1),
        shifted(inner, 1, -1),
        shifted(inner, 2, 1),
        shifted(inner, 2, -1),
    ]


def spread_sum(field, conduct):
    centre = conduct[1:-1]
    total = 0.0
    for value, beside in zip(near(field), near(conduct)):
        total = total + 0.5 * (centre + beside) * value
    return total


def weights(moments):
    m = [moments[i] / moments[0] for i in range(6)]
    g = [m[i] - m[i + 1] for i in range(5)]
    l10 = g[1] / g[0]
    l20 = g[2] / g[0]
    d1 = g[2] - l10 * g[1]
    e = g[3] - l20 * g[1]
    l21 = e / d1
    d2 = g[4] - l20 * g[2] - l21 * e
    y0 = m[0]
    y1 = m[1] - l10 * y0
    y2 = m[2] - l20 * y0 - l21 * y1
    c2 = y2 / d2
    c1 = y1 / d1 - l21 * c2
    c0 = y0 / g[0] - l10 * c1 - l20 * c2
    return c0, c1, c2


def body(forward_field, misfit, receivers, classes, table):
    layers, rows, columns = classes.shape
    sources = lax.axis_size("src")
    per_z = CORES * Y_LO
    depth = sources // per_z
    place = lax.axis_index("src")
    core = place % CORES
    slab = lax.axis_index("slab")
    blocks = depth * CORES
    strip = rows // blocks
    forward = forward_field[0]

    mine = (place // per_z) * CORES + core
    part = lookup(lax.dynamic_slice_in_dim(classes, mine * strip, strip, axis=1), table)
    below = slab_shift(part, 1)
    above = slab_shift(part, -1)
    groups = [
        [z * per_z + y * CORES + c for z in range(depth) for c in range(CORES)] for y in range(Y_LO)
    ]
    halo = lax.all_gather(jnp.stack([below, above]), "src", axis_index_groups=groups)
    halo = jnp.moveaxis(halo, 0, 2).reshape(2, layers, rows, columns)
    conduct = jnp.concatenate([halo[0], lookup(classes, table), halo[1]], axis=0)

    forward_pad = jnp.concatenate(
        [slab_shift(forward[-1:], 1), forward, slab_shift(forward[:1], -1)], axis=0
    )

    pairs = receivers[0].T.astype(jnp.float32)
    entries = jnp.concatenate([pairs, misfit], axis=0)
    entries = jnp.concatenate([slab_shift(entries, 1), entries, slab_shift(entries, -1)], axis=1)
    first = entries[0].astype(jnp.int32) - slab * layers + 3
    inside = (first >= 0) & (first < layers + 6)
    cells = first * (rows * columns) + entries[1].astype(jnp.int32)
    size = (layers + 6) * rows * columns
    right_side = (
        jnp.zeros((size,), jnp.float32)
        .at[jnp.where(inside, cells, size)]
        .add(entries[2], mode="drop")
        .reshape(layers + 6, rows, columns)
    )

    centre = conduct[1:-1]
    diagonal = 0.0
    for beside in near(conduct):
        diagonal = diagonal + 0.5 * (centre + beside)
    layer = jnp.arange(-3, layers + 3) + slab * layers
    real = ((layer >= 0) & (layer < layers * lax.axis_size("slab")))[:, None, None]
    inverse = jnp.where(real, 1.0 / jnp.where(real, diagonal, 1.0), 0.0)
    first_field = right_side * inverse
    spread0 = spread_sum(first_field, conduct[1:-1])
    second_field = spread0 * inverse[1:-1]
    spread1 = spread_sum(second_field, conduct[2:-2])
    third_field = spread1 * inverse[2:-2]
    spread2 = spread_sum(third_field, conduct[3:-3])
    own0, own1, own2 = first_field[3:-3], second_field[2:-2], third_field[1:-1]
    sums = jnp.stack(
        [
            jnp.sum(own0 * right_side[3:-3]),
            jnp.sum(own0 * spread0[2:-2]),
            jnp.sum(own1 * spread0[2:-2]),
            jnp.sum(own1 * spread1[1:-1]),
            jnp.sum(own2 * spread1[1:-1]),
            jnp.sum(own2 * spread2),
        ]
    )
    count = lax.axis_size("slab")
    sums = lax.all_to_all(jnp.broadcast_to(sums, (count, 6)), "slab", 0, 0)
    c0, c1, c2 = weights(jnp.sum(sums, axis=0))
    adjoint = c0 * first_field[2:-2] + c1 * second_field[1:-1] + c2 * third_field
    forward_near = near(forward_pad)
    adjoint_near = near(adjoint)
    adjoint = adjoint[1:-1]
    term = 0.0
    for forward_side, adjoint_side in zip(forward_near, adjoint_near):
        term = term + (forward - forward_side) * (adjoint - adjoint_side)
    term = -0.5 * term

    own = rows // sources
    term = term.reshape(layers, depth * Y_LO, CORES, own, columns)
    term = jnp.transpose(term, (2, 1, 0, 3, 4)).reshape(CORES, depth * Y_LO, layers * own, columns)
    keep = lax.dynamic_index_in_dim(term, core, 0, keepdims=False)
    give = lax.dynamic_index_in_dim(term, 1 - core, 0, keepdims=False)
    got = lax.ppermute(give, "src", [(i, i ^ 1) for i in range(sources)])
    half = keep + got
    groups = [
        [z * per_z + y * CORES + c for z in range(depth) for y in range(Y_LO)] for c in range(CORES)
    ]
    shares = lax.all_to_all(half, "src", 0, 0, axis_index_groups=groups)
    gradient = jnp.sum(shares, axis=0).reshape(layers, own, columns)
    return (adjoint[None], gradient)


def solution(mesh):
    placed = (
        P("src", "slab", None, None),
        P("src", "slab"),
        P("src", "slab", None),
        P("slab", None, None),
        P(),
    )
    return jax.shard_map(
        body,
        mesh=mesh,
        in_specs=placed,
        out_specs=(P("src", "slab", None, None), P("slab", "src", None)),
        check_vma=False,
    )
```

time: 604 us -> 286 us (0.47)
  waiting for transfers between devices: 350 us -> 15.4 us
  blocking collectives: 92.4 us -> 40.1 us
  other arithmetic: 81.3 us -> 124 us
  local copies, waits for them, and re-layouts: 18.3 us -> 52 us
  starting transfers between devices: 39.9 us -> 29.4 us
    unnamed x2 -> x1, waiting for transfers between devices: 234 us -> 0.02 us
    ppermute x10 -> x7, waiting for transfers between devices: 116 us -> 8.98 us  [the longest x6 6.51 us: slab_shift(): return lax.ppermute(value, 'slab', pairs)]
    psum x5 -> x0, blocking collectives: 92.4 us -> none  [the longest x3 52.7 us: norm_sum(): return lax.psum(cells_sum(residual, precond), 'slab')]
    mul x0 -> x3, other arithmetic: none -> 48.4 us  [the longest x1 18.2 us: body(): second_field = spread0 * inverse[1:-1]]
    all_to_all x0 -> x1, blocking collectives: none -> 40.1 us  [body(): shares = lax.all_to_all(half, 'src', 0, 0, axis_index_groups=groups)]
    reduce_sum x7 -> x4, other arithmetic: 49.4 us -> 10.3 us  [the longest x1 6.53 us: body(): jnp.sum(own2 * spread2)]
    slice x4 -> x17, local copies, waits for them, and re-layouts: 1.35 us -> 28 us  [the longest x2 6.79 us: near(): inner = field[1:-1]]
    select_n x1 -> x3, other arithmetic: 0.62 us -> 26.3 us  [the longest x2 24.8 us: lookup(): result = jnp.where(classes == label, table[label], result)]
  transfers between devices with their start and end apart: 11 -> 9, of which waited for: 11 -> 4; matrix products, arithmetic and copies ran while one was open for 3% -> 50% of each run, Pallas kernels for 0% -> 0%
where the time goes in v1:
time: 286 us; the launch traced here: 285 us
  other arithmetic  124 us (43%)
  local copies, waits for them, and re-layouts  52 us (18%)
  blocking collectives  40.1 us (14%)
  starting transfers between devices  29.4 us (10%)
  between operations  23.8 us (8%)
  waiting for transfers between devices  15.4 us (5%)
    all_to_all x1, blocking collectives, body(): shares = lax.all_to_all(half, 'src', 0, 0, axis_index_groups=groups)  40.1 us
    select_n x2, other arithmetic, lookup(): result = jnp.where(classes == label, table[label], result)  24.8 us
    scatter-add x1, other arithmetic, body(): right_side = jnp.zeros((size,), jnp.float32).at[jnp.where(inside, cells,...  24.3 us
    ppermute x6, starting transfers between devices, slab_shift(): return lax.ppermute(value, 'slab', pairs)  20 us
    mul x1, other arithmetic, body(): second_field = spread0 * inverse[1:-1]  18.2 us
    mul x1, other arithmetic, body(): first_field = right_side * inverse  15.8 us
    mul x1, other arithmetic, body(): third_field = spread1 * inverse[2:-2]  14.4 us
    unnamed x25, local copies, waits for them, and re-layouts  8.74 us
  transfers between devices with their start and end apart: 9, of which 4 were waited for; matrix products, arithmetic and copies ran while one was open for 50% of the time, Pallas kernels for 0%

profile of v1, /device:TPU:1, one launch (start us, length us, event | category | flops | bytes accessed | tf_op | source)
XLA Modules:
  0.0 284.6 jit_solution(9968979988669039319)
XLA Ops:
  7.2 0.0 all-gather.3.cloned.1.call-start
  7.2 2.0 fusion.117
  9.2 11.0 %select_select_fusion.1 = f32[4,24,384]{2,1,0:T(8,128)S(1)} fusion(s32[4,384,384]{2,1,0:T(8,128)} %param.8, s32[]{:T(128)S(6)} %select_n.151, f32[]{:T(128)} %bitcast.18, f32[]{:T(128)} %bitcast.17, f32[]{:T(128)} %bitcast.16, f32[]{:T(128)} %bitcast.15, f32[]{:T(128)} %bitcast.14, f32[]{:T(128)} %bitcast.13, f32[]{:T(128)} %bitcast.12, f32[]{:T(128)} %bitcast.11, ...), kind=kLoop, calls=%fused_computation.176 | loop fusion | flops 1179648 | bytes 294980 | tf_op jit(solution)/shard_map/jit(_where)/select_n | solution.py:13
  20.3 5.7 %collective-permute-start.2 = (f32[4,24,384]{2,1,0:T(8,128)S(1)}, f32[4,24,384]{2,1,0:T(8,128)S(1)}, u32[]{:S(2)}, u32[]{:S(2)}) collective-permute-start(f32[4,24,384]{2,1,0:T(8,128)S(1)} %select_select_fusion.1), channel_id=1, source_target_pairs={{0,1},{1,2},{2,3},{3,4},{4,5},{5,6},{6,7},{8,9},{9,10},{10,11},{11... | collective-permute-start | bytes 442376 | tf_op jit(solution)/shard_map/ppermute | solution.py:20
  25.9 1.3 collective-permute-start.3
  27.2 1.2 collective-permute-done.2
  28.4 5.3 %collective-permute-done.3 = f32[4,24,384]{2,1,0:T(8,128)S(1)} collective-permute-done((f32[4,24,384]{2,1,0:T(8,128)S(1)}, f32[4,24,384]{2,1,0:T(8,128)S(1)}, u32[]{:S(2)}, u32[]{:S(2)}) %collective-permute-start.3) | collective-permute-done | bytes 147488 | tf_op jit(solution)/shard_map/ppermute | solution.py:20
  33.7 0.7 pad_maximum_fusion.5
  34.4 0.0 all-gather.3.cloned.1.call-update
  34.5 0.7 convert_bitcast_fusion
  35.2 1.3 pad_maximum_fusion.6
  36.5 4.4 %collective-permute-start = (f32[3,1152]{1,0:T(4,128)}, f32[3,1152]{1,0:T(4,128)}, u32[]{:S(2)}, u32[]{:S(2)}) collective-permute-start(f32[3,1152]{1,0:T(4,128)} %pad_maximum_fusion.6), channel_id=1, source_target_pairs={{0,1},{1,2},{2,3},{3,4},{4,5},{5,6},{6,7},{8,9},{9,10},{10,11},{11... | collective-permute-start | bytes 41480 | tf_op jit(solution)/shard_map/ppermute | solution.py:20
  40.9 1.3 collective-permute-start.1
  42.1 2.3 slice_bitcast_fusion.1
  44.5 1.3 collective-permute-start.4
  45.8 6.2 %collective-permute-start.5 = (f32[1,384,384]{2,1,0:T(8,128)}, f32[1,384,384]{2,1,0:T(8,128)S(1)}, u32[]{:S(2)}, u32[]{:S(2)}) collective-permute-start(f32[1,384,384]{2,1,0:T(8,128)} %get-tuple-element.35), channel_id=1, source_target_pairs={{0,1},{1,2},{2,3},{3,4},{4,5},{5,6},{6,7},{8,9},{9,10},{10,11},{11... | collective-permute-start | bytes 1769480 | tf_op jit(solution)/shard_map/ppermute | solution.py:20
  51.9 13.7 %select_select_fusion = f32[4,384,384]{2,1,0:T(8,128)S(1)} fusion(s32[4,384,384]{2,1,0:T(8,128)} %param.8, f32[]{:T(128)} %bitcast.18, f32[]{:T(128)} %bitcast.17, f32[]{:T(128)} %bitcast.16, f32[]{:T(128)} %bitcast.15, f32[]{:T(128)} %bitcast.14, f32[]{:T(128)} %bitcast.13, f32[]{:T(128)} %bitcast.12, f32[]{:T(128)} %bitcast.11, f32[]{:T(128)} %bitcast.10, ...), kind=kLoop, calls=%fused_computation.169 | loop fusion | flops 18874368 | bytes 4718656 | tf_op jit(solution)/shard_map/jit(_where)/select_n | solution.py:13
  65.7 0.0 copy-start.3
  65.7 1.5 fusion.107
  67.2 1.5 fusion.106
  68.7 24.3 %scatter_custom_fusion = f32[1474560]{0:T(1024)} fusion(s32[3456]{0:T(1024)} %fusion.106, f32[3456]{0:T(1024)} %fusion.107, f32[]{:T(128)} %constant.30.clone.1), kind=kCustom, calls=%fused_computation.102 | custom fusion | flops 3456 | bytes 5898752 | tf_op jit(solution)/shard_map/scatter-add | solution.py:108
  93.0 7.2 %reshape.110 = f32[10,384,384]{2,1,0:T(8,128)} reshape(f32[1474560]{0:T(1024)} %scatter_custom_fusion) | data formatting | bytes 11796480 | tf_op jit(solution)/shard_map/reshape | solution.py:109
  100.3 3.3 %slice.470 = f32[589824]{0:T(1024)} slice(f32[1474560]{0:T(1024)} %scatter_custom_fusion), slice={[442368:1032192]} | slice | bytes 4718592 | tf_op jit(solution)/shard_map/slice | solution.py:128
  103.5 3.4 %slice.393 = f32[4,384,384]{2,1,0:T(8,128)} reshape(f32[589824]{0:T(1024)} %slice.470) | data formatting | bytes 4718592 | tf_op jit(solution)/shard_map/slice | solution.py:128
  106.9 2.7 fusion.115
  109.6 0.2 copy.39
  109.8 0.2 copy.40
  109.9 1.6 copy-done.7
  111.5 0.5 pad_maximum_fusion
  112.1 3.2 %slice.466 = f32[10,384,384]{2,1,0:T(8,128)} slice(f32[12,384,384]{2,1,0:T(8,128)S(1)} %pad_maximum_fusion), slice={[1:11], [0:384], [0:384]} | slice | bytes 11796480 | tf_op jit(solution)/shard_map/slice | solution.py:112
  115.3 1.5 copy-done
  116.8 15.8 %fusion.113 = (f32[10,384,384]{2,1,0:T(8,128)S(1)}, f32[10,384,384]{2,1,0:T(8,128)}) fusion(f32[10,384,384]{2,1,0:T(8,128)} %reshape.110, f32[10,384,384]{2,1,0:T(8,128)} %slice.466, f32[12,384,384]{2,1,0:T(8,128)S(1)} %pad_maximum_fusion, pred[10]{0:T(512)(128)(4,1)S(1)} %compare_and_fusion), kind=kLoop, calls=%fused_computation.195 | loop fusion | flops 23592960 | bytes 35389448 | tf_op jit(solution)/shard_map/mul | solution.py:119
  132.6 2.6 slice.476
  135.2 3.1 %slice-done = f32[8,384,384]{2,1,0:T(8,128)S(1)} async-done(((f32[12,384,384]{2,1,0:T(8,128)}), f32[8,384,384]{2,1,0:T(8,128)S(1)}, s32[]{:S(2)}) %slice-start) | async-done | bytes 4718616 | tf_op jit(solution)/shard_map/slice | solution.py:46
  138.3 18.2 %slice_multiply_fusion = (f32[8,384,384]{2,1,0:T(8,128)}, f32[8,384,384]{2,1,0:T(8,128)}) fusion(f32[10,384,384]{2,1,0:T(8,128)} %get-tuple-element.27, f32[8,384,384]{2,1,0:T(8,128)} %slice.476, f32[8,384,384]{2,1,0:T(8,128)S(1)} %slice-done, f32[10,384,384]{2,1,0:T(8,128)S(1)} %get-tuple-element.26, f32[12,384,384]{2,1,0:T(8,128)} %copy-done), kind=kLoop, calls=%fused_computation.45 | loop fusion | flops 28311552 | bytes 42467328 | tf_op jit(solution)/shard_map/mul | solution.py:121
  156.5 4.2 %slice.487 = f32[6,384,384]{2,1,0:T(8,128)} slice(f32[8,384,384]{2,1,0:T(8,128)} %get-tuple-element.24), slice={[1:7], [0:384], [0:384]} | slice | bytes 7077888 | tf_op jit(solution)/shard_map/slice | solution.py:34
  160.8 14.4 %slice_multiply_fusion.4 = (f32[6,384,384]{2,1,0:T(8,128)S(1)}, f32[6,384,384]{2,1,0:T(8,128)}) fusion(f32[10,384,384]{2,1,0:T(8,128)} %get-tuple-element.27, f32[6,384,384]{2,1,0:T(8,128)} %slice.487, f32[6,384,384]{2,1,0:T(8,128)S(1)} %slice-done.1, f32[8,384,384]{2,1,0:T(8,128)} %get-tuple-element.24, f32[4,384,384]{2,1,0:T(8,128)} %copy-done.3, ...), kind=kLoop, calls=%fused_computation.93 | loop fusion | flops 23003136 | bytes 31850496 | tf_op jit(solution)/shard_map/mul | solution.py:123
  175.1 0.0 copy-start.4
  175.2 0.2 slice.490
  175.3 2.8 copy-done.4
  178.1 0.7 copy-done.6
  178.8 6.5 %fusion.105 = (f32[]{:T(128)}, f32[]{:T(128)}) fusion(f32[4,384,384]{2,1,0:T(8,128)S(1)} %slice.490, f32[4,384,384]{2,1,0:T(8,128)S(1)} %copy-done.4, f32[6,384,384]{2,1,0:T(8,128)S(1)} %get-tuple-element.22, f32[4,384,384]{2,1,0:T(8,128)S(1)} %bitcast.61, f32[4,384,384]{2,1,0:T(8,128)} %bitcast.64, f32[6,384,384]{2,1,0:T(8,128)} %get-tuple-element.23), kind=kLoop, calls=%fused_computation.170 | loop fusion | flops 17104894 | bytes 18874376 | tf_op jit(solution)/shard_map/reduce_sum | solution.py:133
  185.4 3.7 %multiply_reduce_fusion.1 = (f32[]{:T(128)}, f32[]{:T(128)}, f32[]{:T(128)}, f32[]{:T(128)}) fusion(f32[6,384,384]{2,1,0:T(8,128)S(1)} %copy-done.8, f32[8,384,384]{2,1,0:T(8,128)S(1)} %bitcast.58, f32[8,384,384]{2,1,0:T(8,128)} %get-tuple-element.25, f32[4,384,384]{2,1,0:T(8,128)} %slice.393, f32[10,384,384]{2,1,0:T(8,128)S(1)} %get-tuple-element.26), kind=kLoop, calls=%fused_computation.165 | loop fusion | flops 4718588 | bytes 11796496 | tf_op jit(solution)/shard_map/reduce_sum | solution.py:131
  189.0 3.9 %stack.39 = f32[6]{0:T(128)S(1)} concatenate(f32[1]{0:T(128)} %bitcast.26, f32[1]{0:T(128)} %bitcast.27, f32[1]{0:T(128)} %bitcast.28, f32[1]{0:T(128)} %bitcast.29, f32[1]{0:T(128)} %bitcast.30, f32[1]{0:T(128)} %bitcast.31), dimensions={0} | concatenate | bytes 48 | tf_op jit(solution)/shard_map/stack | solution.py:126
  193.0 0.6 broadcast_in_dim.173
  193.6 4.8 %all-to-all-start = ((f32[8,1,6]{2,1,0:T(1,128)}), f32[8,1,6]{2,1,0:T(1,128)S(1)}, u32[]{:S(2)}, u32[]{:S(2)}) async-start(f32[8,1,6]{2,1,0:T(1,128)} %broadcast_in_dim.173), calls=%async_computation | async-start | bytes 8192 | tf_op jit(solution)/shard_map/all_to_all | solution.py:137
  198.4 6.4 %all-to-all-done = f32[8,1,6]{2,1,0:T(1,128)S(1)} async-done(((f32[8,1,6]{2,1,0:T(1,128)}), f32[8,1,6]{2,1,0:T(1,128)S(1)}, u32[]{:S(2)}, u32[]{:S(2)}) %all-to-all-start) | async-done | bytes 224 | tf_op jit(solution)/shard_map/all_to_all | solution.py:137
  204.8 0.7 fusion.116
  214.9 4.7 %fusion.58 = f32[6,384,384]{2,1,0:T(8,128)S(1)} fusion(f32[10,384,384]{2,1,0:T(8,128)} %copy-done.1, f32[6,384,384]{2,1,0:T(8,128)} %copy-done.2, f32[]{:T(128)S(6)} %div.66, f32[]{:T(128)S(6)} %sub.117, f32[]{:T(128)S(6)} %sub.119, f32[8,384,384]{2,1,0:T(8,128)} %get-tuple-element.24), kind=kLoop, calls=%fused_computation.92 | loop fusion | flops 4423680 | bytes 14155788 | tf_op jit(solution)/shard_map/add | solution.py:139
  219.6 0.0 copy-start.9
  219.6 0.2 slice.494
  219.8 0.0 collective-permute-done.5
  219.8 1.5 copy-done.9
  221.3 4.8 %fusion.78 = (f32[4,384,384]{2,1,0:T(8,128)S(1)}, f32[1,4,384,384]{3,2,1,0:T(8,128)}) fusion(f32[4,384,384]{2,1,0:T(8,128)S(1)} %bitcast.67, f32[4,384,384]{2,1,0:T(8,128)S(1)} %slice.494, f32[6,384,384]{2,1,0:T(8,128)S(1)} %fusion.58, f32[1,384,384]{2,1,0:T(8,128)S(1)} %collective-permute-done.5, f32[1,384,384]{2,1,0:T(8,128)S(1)} %collective-permute-done.4), kind=kLoop, calls=%fused_computation.129 | loop fusion | flops 15335424 | bytes 17694720 | tf_op jit(solution)/shard_map/mul | solution.py:146
  226.1 1.5 copy.42
  227.6 1.4 copy.43
  229.0 0.2 constant_dynamic-slice_fusion
  229.1 0.4 copy.56
  229.5 4.5 %collective-permute-start.6 = (f32[16,48,384]{2,1,0:T(8,128)S(1)}, f32[16,48,384]{2,1,0:T(8,128)S(1)}, u32[]{:S(2)}, u32[]{:S(2)}) collective-permute-start(f32[16,48,384]{2,1,0:T(8,128)S(1)} %bitcast.69), channel_id=1, source_target_pairs={{0,8},{8,0},{16,24},{24,16},{32,40},{40,32},{48,56},{56,48},{64,72... | collective-permute-start | bytes 3538952 | tf_op jit(solution)/shard_map/ppermute | solution.py:153
  234.1 2.5 collective-permute-done.6
  236.5 0.4 bitcast_add_fusion
  236.9 40.1 %all_to_all.11 = f32[16,48,384]{2,1,0:T(8,128)S(1)} all-to-all(f32[16,48,384]{2,1,0:T(8,128)S(1)} %bitcast_add_fusion), channel_id=1, replica_groups={{0,16,32,48,64,80,96,112,128,144,160,176,192,208,224,240},{8,24,40,56,7..., dimensions={0} | all-to-all | bytes 2359296 | tf_op jit(solution)/shard_map/all_to_all | solution.py:158
  277.0 0.1 reduce_sum.79
  277.1 0.7 copy.46
  (27 shorter events, 0.1 us)
Async XLA Ops:
  7.2 99.7 %all-gather.3.cloned.1.call-start = ((), (), s32[]{:S(2)}) async-start(), calls=%async_computation.2 | async-start | bytes 5013504 | tf_op jit(solution)/shard_map/all_gather | solution.py:90
  20.3 8.2 %collective-permute-start.2 = (f32[4,24,384]{2,1,0:T(8,128)S(1)}, f32[4,24,384]{2,1,0:T(8,128)S(1)}, u32[]{:S(2)}, u32[]{:S(2)}) collective-permute-start(f32[4,24,384]{2,1,0:T(8,128)S(1)} %select_select_fusion.1), channel_id=1, source_target_pairs={{0,1},{1,2},{2,3},{3,4},{4,5},{5,6},{6,7},{8,9},{9,10},{10,11},{11... | collective-permute-start | bytes 442376 | tf_op jit(solution)/shard_map/ppermute | solution.py:20
  25.9 7.8 %collective-permute-start.3 = (f32[4,24,384]{2,1,0:T(8,128)S(1)}, f32[4,24,384]{2,1,0:T(8,128)S(1)}, u32[]{:S(2)}, u32[]{:S(2)}) collective-permute-start(f32[4,24,384]{2,1,0:T(8,128)S(1)} %select_select_fusion.1), channel_id=1, source_target_pairs={{1,0},{2,1},{3,2},{4,3},{5,4},{6,5},{7,6},{9,8},{10,9},{11,10},{12... | collective-permute-start | bytes 442376 | tf_op jit(solution)/shard_map/ppermute | solution.py:20
  36.5 29.2 %collective-permute-start = (f32[3,1152]{1,0:T(4,128)}, f32[3,1152]{1,0:T(4,128)}, u32[]{:S(2)}, u32[]{:S(2)}) collective-permute-start(f32[3,1152]{1,0:T(4,128)} %pad_maximum_fusion.6), channel_id=1, source_target_pairs={{0,1},{1,2},{2,3},{3,4},{4,5},{5,6},{6,7},{8,9},{9,10},{10,11},{11... | collective-permute-start | bytes 41480 | tf_op jit(solution)/shard_map/ppermute | solution.py:20
  40.9 24.8 %collective-permute-start.1 = (f32[3,1152]{1,0:T(4,128)}, f32[3,1152]{1,0:T(4,128)}, u32[]{:S(2)}, u32[]{:S(2)}) collective-permute-start(f32[3,1152]{1,0:T(4,128)} %pad_maximum_fusion.6), channel_id=1, source_target_pairs={{1,0},{2,1},{3,2},{4,3},{5,4},{6,5},{7,6},{9,8},{10,9},{11,10},{12... | collective-permute-start | bytes 41480 | tf_op jit(solution)/shard_map/ppermute | solution.py:20
  44.5 175.3 %collective-permute-start.4 = (f32[1,384,384]{2,1,0:T(8,128)}, f32[1,384,384]{2,1,0:T(8,128)S(1)}, u32[]{:S(2)}, u32[]{:S(2)}) collective-permute-start(f32[1,384,384]{2,1,0:T(8,128)} %get-tuple-element.34), channel_id=1, source_target_pairs={{1,0},{2,1},{3,2},{4,3},{5,4},{6,5},{7,6},{9,8},{10,9},{11,10},{12... | collective-permute-start | bytes 1769480 | tf_op jit(solution)/shard_map/ppermute | solution.py:20
  45.8 174.0 %collective-permute-start.5 = (f32[1,384,384]{2,1,0:T(8,128)}, f32[1,384,384]{2,1,0:T(8,128)S(1)}, u32[]{:S(2)}, u32[]{:S(2)}) collective-permute-start(f32[1,384,384]{2,1,0:T(8,128)} %get-tuple-element.35), channel_id=1, source_target_pairs={{0,1},{1,2},{2,3},{3,4},{4,5},{5,6},{6,7},{8,9},{9,10},{10,11},{11... | collective-permute-start | bytes 1769480 | tf_op jit(solution)/shard_map/ppermute | solution.py:20
  65.7 44.3 %copy-start.3 = (f32[4,384,384]{2,1,0:T(8,128)}, f32[4,384,384]{2,1,0:T(8,128)S(1)}, u32[]{:S(2)}) copy-start(f32[4,384,384]{2,1,0:T(8,128)S(1)} %select_select_fusion) | copy-start | bytes 7077892
  109.8 2.3 copy-start.5
  109.9 1.6 copy-start.7
  112.1 4.7 %copy-start = (f32[12,384,384]{2,1,0:T(8,128)}, f32[12,384,384]{2,1,0:T(8,128)S(1)}, u32[]{:S(2)}) copy-start(f32[12,384,384]{2,1,0:T(8,128)S(1)} %pad_maximum_fusion) | copy-start | bytes 21233668
  132.6 52.8 %copy-start.1 = (f32[10,384,384]{2,1,0:T(8,128)}, f32[10,384,384]{2,1,0:T(8,128)S(1)}, u32[]{:S(2)}) copy-start(f32[10,384,384]{2,1,0:T(8,128)S(1)} %get-tuple-element.26) | copy-start | bytes 17694724
  132.6 5.7 %slice-start = ((f32[12,384,384]{2,1,0:T(8,128)}), f32[8,384,384]{2,1,0:T(8,128)S(1)}, s32[]{:S(2)}) async-start(f32[12,384,384]{2,1,0:T(8,128)} %copy-done), calls=%async_computation.3 | async-start | bytes 9437184 | tf_op jit(solution)/shard_map/slice | solution.py:46
  156.5 4.2 %slice-start.1 = ((f32[12,384,384]{2,1,0:T(8,128)}), f32[6,384,384]{2,1,0:T(8,128)S(1)}, s32[]{:S(2)}) async-start(f32[12,384,384]{2,1,0:T(8,128)} %copy-done), calls=%async_computation.4 | async-start | bytes 7077888 | tf_op jit(solution)/shard_map/slice | solution.py:46
  175.1 10.2 %copy-start.2 = (f32[6,384,384]{2,1,0:T(8,128)}, f32[6,384,384]{2,1,0:T(8,128)S(1)}, u32[]{:S(2)}) copy-start(f32[6,384,384]{2,1,0:T(8,128)S(1)} %get-tuple-element.22) | copy-start | bytes 10616836
  175.1 2.9 %copy-start.4 = (f32[4,384,384]{2,1,0:T(8,128)S(1)}, f32[4,384,384]{2,1,0:T(8,128)}, u32[]{:S(2)}) copy-start(f32[4,384,384]{2,1,0:T(8,128)} %copy-done.3) | copy-start | bytes 7077892
  175.1 3.6 %copy-start.6 = (f32[1,4,16,24,384]{4,3,2,1,0:T(8,128)S(1)}, f32[1,4,16,24,384]{4,3,2,1,0:T(8,128)}, u32[]{:S(2)}) copy-start(f32[1,4,16,24,384]{4,3,2,1,0:T(8,128)} %copy-done.5) | copy-start | bytes 7077892
  175.2 10.2 %slice-start.2 = ((s8[4718592]{0:T(1024)(128)(4,1)}), s8[4194304]{0:T(1024)(128)(4,1)S(1)}, s32[]{:S(2)}) async-start(s8[4718592]{0:T(1024)(128)(4,1)} %bitcast.57), calls=%async_computation.5 | async-start | bytes 8388608
  178.8 6.5 %slice-start.3 = ((s8[4718592]{0:T(1024)(128)(4,1)}), s8[524288]{0:T(1024)(128)(4,1)S(1)}, s32[]{:S(2)}) async-start(s8[4718592]{0:T(1024)(128)(4,1)} %bitcast.57), calls=%async_computation.6 | async-start | bytes 1048576
  178.8 6.5 %copy-start.8 = (f32[6,384,384]{2,1,0:T(8,128)S(1)}, f32[6,384,384]{2,1,0:T(8,128)}, u32[]{:S(2)}) copy-start(f32[6,384,384]{2,1,0:T(8,128)} %get-tuple-element.23) | copy-start | bytes 10616836
  193.6 11.2 %all-to-all-start = ((f32[8,1,6]{2,1,0:T(1,128)}), f32[8,1,6]{2,1,0:T(1,128)S(1)}, u32[]{:S(2)}, u32[]{:S(2)}) async-start(f32[8,1,6]{2,1,0:T(1,128)} %broadcast_in_dim.173), calls=%async_computation | async-start | bytes 8192 | tf_op jit(solution)/shard_map/all_to_all | solution.py:137
  219.6 1.7 copy-start.9
  229.5 7.0 %collective-permute-start.6 = (f32[16,48,384]{2,1,0:T(8,128)S(1)}, f32[16,48,384]{2,1,0:T(8,128)S(1)}, u32[]{:S(2)}, u32[]{:S(2)}) collective-permute-start(f32[16,48,384]{2,1,0:T(8,128)S(1)} %bitcast.69), channel_id=1, source_target_pairs={{0,8},{8,0},{16,24},{24,16},{32,40},{40,32},{48,56},{56,48},{64,72... | collective-permute-start | bytes 3538952 | tf_op jit(solution)/shard_map/ppermute | solution.py:153
Sparse Core Ops, SparseCore 0:
  34.6 46.5 all-gather.2

commit v2 on v1

v2 whole, which is shorter than its diff:
```python
import jax
import jax.numpy as jnp
from jax import lax
from jax.experimental import pallas as pl
from jax.experimental.pallas import tpu as pltpu
from jax.sharding import PartitionSpec as P

CORES = 2
Y_LO = 2
REACH = 3
PAD = 8
ROWS = 96
GROUP = 4
VMEM = 56 * 1024 * 1024


def lookup(classes, table):
    labels = jnp.arange(table.shape[0], dtype=jnp.int32)[:, None, None, None]
    return jnp.sum(jnp.where(classes[None] == labels, table[:, None, None, None], 0.0), axis=0)


def slab_shift(value, step):
    count = lax.axis_size("slab")
    pairs = [(i, i + step) for i in range(count) if 0 <= i + step < count]
    return lax.ppermute(value, "slab", pairs)


def scatter_kernel(below, own, above, classes, table, side, conduct):
    layers, rows, columns = classes.shape
    slab = lax.axis_index("slab")
    count = own.shape[1]
    across = lax.broadcasted_iota(jnp.int32, (columns, count), 0)
    down = lax.broadcasted_iota(jnp.int32, (rows, count), 0)
    sources = (
        (below, range(layers - REACH, layers), 0),
        (own, range(layers), REACH),
        (above, range(REACH), REACH + layers),
    )
    for number, (entries, planes, start) in enumerate(sources):
        first = entries[0:1, :] - ((slab + number - 1) * layers).astype(jnp.float32)
        index = entries[1:2, :]
        value = entries[2:3, :]
        line = jnp.floor((index + 0.5) * (1.0 / columns))
        column = (index - line * columns).astype(jnp.int32)
        place = (first * rows + line).astype(jnp.int32)
        hit = across == column
        parts = []
        rest = value
        for _ in range(3):
            piece = rest.astype(jnp.bfloat16)
            rest = rest - piece.astype(jnp.float32)
            parts.append(jnp.where(hit, piece.astype(jnp.float32), 0.0).astype(jnp.bfloat16))
        for step, plane in enumerate(planes):
            chosen = jnp.where(down + plane * rows == place, 1.0, 0.0).astype(jnp.bfloat16)
            total = 0.0
            for part in parts:
                total = total + lax.dot_general(
                    chosen, part, (((1,), (1,)), ((), ())), preferred_element_type=jnp.float32
                )
            side[start + step] = total

    values = [table[label] for label in range(table.shape[0])]

    def strip(at, carry):
        at = pl.multiple_of(at * ROWS, ROWS)
        for layer in range(layers):
            conduct[layer, pl.ds(at, ROWS), :] = choose(classes[layer, pl.ds(at, ROWS), :], values)
        return carry

    lax.fori_loop(0, rows // ROWS, strip, 0)


def choose(labels, values):
    bit = 1
    while len(values) > 1:
        high = (labels & bit) != 0
        values = [jnp.where(high, values[i + 1], values[i]) for i in range(0, len(values), 2)]
        bit *= 2
    return values[0]


def vectors_kernel(own, halo, side, out0, out1, out2, sums, cond, near_x, near_y, near_z, inverse, f0, f1, f2, marks):
    layers, rows, columns = own.shape
    blocks, _, _, strip, _ = halo.shape
    filled = pl.ds(PAD, rows)
    copies = [
        pltpu.make_async_copy(own, cond.at[pl.ds(layers, layers), filled], marks.at[0])
    ]
    for block in range(blocks):
        for step in range(2):
            target = cond.at[pl.ds(2 * step * layers, layers), pl.ds(PAD + block * strip, strip)]
            copies.append(
                pltpu.make_async_copy(halo.at[block, step], target, marks.at[len(copies)])
            )
    for copy in copies:
        copy.start()
    slab = lax.axis_index("slab")
    slabs = lax.axis_size("slab")
    deep = layers + 2 * REACH
    lane = lax.broadcasted_iota(jnp.int32, (ROWS, columns), 1)
    blank = jnp.zeros((PAD, columns), jnp.float32)
    for ref in (cond, near_y, f0, f1, f2):
        for plane in range(ref.shape[0]):
            ref[plane, 0:PAD, :] = blank
            ref[plane, PAD + rows : 2 * PAD + rows, :] = blank
    for copy in copies:
        copy.wait()

    def here(at):
        return pl.ds(pl.multiple_of(at * ROWS + PAD, PAD), ROWS)

    def before(at):
        return pl.ds(pl.multiple_of(at * ROWS, PAD), ROWS + PAD)

    def after(at):
        return pl.ds(pl.multiple_of(at * ROWS + PAD, PAD), ROWS + PAD)

    def plain(at):
        return pl.ds(pl.multiple_of(at * ROWS, ROWS), ROWS)

    strips = rows // ROWS

    def setup(plane, carry):
        layer = slab * layers + plane - REACH
        real = jnp.logical_and(layer >= 0, layer < slabs * layers)
        scale = jnp.where(real, 1.0, 0.0)

        def step(at, inner):
            centre = cond[plane + 1, here(at), :]
            lower = cond[plane, here(at), :]
            upper = cond[plane + 2, here(at), :]
            ahead = cond[plane + 1, after(at), :][1 : ROWS + 1]
            behind = cond[plane + 1, before(at), :][PAD - 1 : PAD - 1 + ROWS]
            right = jnp.where(lane == columns - 1, 0.0, pltpu.roll(centre, columns - 1, 1))
            left = jnp.where(lane == 0, 0.0, pltpu.roll(centre, 1, 1))
            total = 6.0 * centre + ((lower + upper) + (ahead + behind) + (left + right))
            turned = (2.0 * scale) / (total + (1.0 - scale))
            inverse[plane, plain(at), :] = turned
            near_x[plane, plain(at), :] = jnp.where(lane == columns - 1, 0.0, 0.5 * (centre + right))
            near_y[plane, here(at), :] = 0.5 * (centre + ahead)
            near_z[plane, plain(at), :] = 0.5 * (centre + upper)
            f0[plane, here(at), :] = side[plane, plain(at), :] * turned
            return inner

        return lax.fori_loop(0, strips, step, carry)

    lax.fori_loop(0, deep, setup, 0)
    thick = layers + 2
    write0 = pltpu.make_async_copy(f0.at[pl.ds(2, thick), filled], out0, marks.at[0])
    write0.start()

    def spread(field, offset, plane, at):
        centre = field[plane, here(at), :]
        across = near_x[plane + offset, plain(at), :]
        total = across * pltpu.roll(centre, columns - 1, 1) + pltpu.roll(across * centre, 1, 1)
        ahead = field[plane, after(at), :][1 : ROWS + 1]
        total = total + near_y[plane + offset, here(at), :] * ahead
        behind = near_y[plane + offset, before(at), :] * field[plane, before(at), :]
        total = total + behind[PAD - 1 : PAD - 1 + ROWS]
        total = total + near_z[plane + offset, plain(at), :] * field[plane + 1, here(at), :]
        total = total + near_z[plane + offset - 1, plain(at), :] * field[plane - 1, here(at), :]
        return centre, total

    def fold(value):
        total = value[0:8]
        for start in range(8, ROWS, 8):
            total = total + value[start : start + 8]
        return total

    def outer(field, offset, target, planes):
        for plane in planes:

            def step(at, inner, plane=plane):
                _, total = spread(field, offset, plane, at)
                target[plane - 1, here(at), :] = total * inverse[plane + offset, plain(at), :]
                return inner

            lax.fori_loop(0, strips, step, 0)

    zero = jnp.zeros((8, columns), jnp.float32)

    def inside0(plane, carry):
        def step(at, inner):
            s0, s1, s2 = inner
            centre, total = spread(f0, 0, plane, at)
            value = total * inverse[plane, plain(at), :]
            f1[plane - 1, here(at), :] = value
            return (
                s0 + fold(centre * side[plane, plain(at), :]),
                s1 + fold(centre * total),
                s2 + fold(value * total),
            )

        return lax.fori_loop(0, strips, step, carry)

    def inside1(plane, carry):
        def step(at, inner):
            s3, s4 = inner
            centre, total = spread(f1, 1, plane, at)
            value = total * inverse[plane + 1, plain(at), :]
            f2[plane - 1, here(at), :] = value
            return s3 + fold(centre * total), s4 + fold(value * total)

        return lax.fori_loop(0, strips, step, carry)

    def inside2(plane, carry):
        def step(at, inner):
            centre, total = spread(f2, 2, plane, at)
            return inner + fold(centre * total)

        return lax.fori_loop(0, strips, step, carry)

    outer(f0, 0, f1, (1, 2, deep - 3, deep - 2))
    s0, s1, s2 = lax.fori_loop(REACH, REACH + layers, inside0, (zero, zero, zero))
    write1 = pltpu.make_async_copy(f1.at[pl.ds(1, thick), filled], out1, marks.at[1])
    write1.start()
    outer(f1, 1, f2, (1, deep - 4))
    s3, s4 = lax.fori_loop(REACH - 1, REACH - 1 + layers, inside1, (zero, zero))
    write2 = pltpu.make_async_copy(f2.at[:, filled], out2, marks.at[2])
    write2.start()
    s5 = lax.fori_loop(REACH - 2, REACH - 2 + layers, inside2, zero)
    for row, total in enumerate((s0, s1, s2, s3, s4, s5)):
        single = jnp.sum(jnp.sum(total, axis=0, keepdims=True), axis=1, keepdims=True)
        sums[row : row + 1, :] = jnp.broadcast_to(single, (1, sums.shape[1]))
    sums[6:8, :] = jnp.zeros((2, sums.shape[1]), jnp.float32)
    for copy in (write0, write1, write2):
        copy.wait()


def weights(moments):
    m = [moments[i] / moments[0] for i in range(6)]
    g = [m[i] - m[i + 1] for i in range(5)]
    l10 = g[1] / g[0]
    l20 = g[2] / g[0]
    d1 = g[2] - l10 * g[1]
    e = g[3] - l20 * g[1]
    l21 = e / d1
    d2 = g[4] - l20 * g[2] - l21 * e
    y0 = m[0]
    y1 = m[1] - l10 * y0
    y2 = m[2] - l20 * y0 - l21 * y1
    c2 = y2 / d2
    c1 = y1 / d1 - l21 * c2
    c0 = y0 / g[0] - l10 * c1 - l20 * c2
    return c0, c1, c2


def terms_kernel(sums, w0, w1, w2, forward, lower, upper, adjoint, keep, give, adj, fwd):
    layers, rows, columns = forward.shape
    pairs, _, _ = keep.shape
    strip = rows // pairs
    half = strip // 2
    first = lax.axis_index("src") % CORES == 0
    blank = jnp.zeros((PAD, columns), jnp.float32)
    for ref in (adj, fwd):
        for plane in range(layers + 2):
            ref[plane, 0:PAD, :] = blank
            ref[plane, PAD + rows : 2 * PAD + rows, :] = blank
    fwd[0, PAD : PAD + rows, :] = lower[0]
    fwd[layers + 1, PAD : PAD + rows, :] = upper[0]
    total = sums[0]
    for other in range(1, sums.shape[0]):
        total = total + sums[other]
    c0, c1, c2 = weights([total[i : i + 1, 0:1] for i in range(6)])
    c0, c1, c2 = [jnp.broadcast_to(c, (ROWS, columns)) for c in (c0, c1, c2)]

    for plane in range(layers + 2):

        def mix(at, carry, plane=plane):
            span = pl.ds(pl.multiple_of(at * ROWS, ROWS), ROWS)
            wide = pl.ds(pl.multiple_of(at * ROWS + PAD, PAD), ROWS)
            value = c0 * w0[plane, span, :] + c1 * w1[plane, span, :] + c2 * w2[plane, span, :]
            adj[plane, wide, :] = value
            if 0 < plane <= layers:
                adjoint[plane - 1, span, :] = value
                fwd[plane, wide, :] = forward[plane - 1, span, :]
            return carry

        lax.fori_loop(0, rows // ROWS, mix, 0)

    tall = strip * GROUP
    lane = lax.broadcasted_iota(jnp.int32, (tall, columns), 1)
    last = lane == columns - 1
    start = lane == 0

    def ahead(value):
        return jnp.where(last, 0.0, pltpu.roll(value, columns - 1, 1))

    for layer in range(layers):

        def step(at, carry, layer=layer):
            wide = pl.ds(pl.multiple_of(at * tall + PAD, PAD), tall)
            more = pl.ds(pl.multiple_of(at * tall, PAD), tall + 2 * PAD)
            f_all = fwd[layer + 1, more, :]
            a_all = adj[layer + 1, more, :]
            f = f_all[PAD : PAD + tall]
            a = a_all[PAD : PAD + tall]
            edge = (f - ahead(f)) * (a - ahead(a))
            value = edge + jnp.where(start, f * a, pltpu.roll(edge, 1, 1))
            for plane in (layer, layer + 2):
                value = value + (f - fwd[plane, wide, :]) * (a - adj[plane, wide, :])
            for shift in (PAD - 1, PAD + 1):
                span = slice(shift, shift + tall)
                value = value + (f - f_all[span]) * (a - a_all[span])
            value = -0.5 * value
            for number in range(GROUP):
                top = value[number * strip : number * strip + half]
                bottom = value[number * strip + half : (number + 1) * strip]
                block = at * GROUP + number
                keep[block, layer * half : (layer + 1) * half, :] = jnp.where(first, top, bottom)
                give[block, layer * half : (layer + 1) * half, :] = jnp.where(first, bottom, top)
            return carry

        lax.fori_loop(0, pairs // GROUP, step, 0)


def body(forward_field, misfit, receivers, classes, table):
    layers, rows, columns = classes.shape
    sources = lax.axis_size("src")
    count = lax.axis_size("slab")
    per_z = CORES * Y_LO
    depth = sources // per_z
    place = lax.axis_index("src")
    core = place % CORES
    blocks = depth * CORES
    strip = rows // blocks
    forward = forward_field[0]
    params = pltpu.CompilerParams(vmem_limit_bytes=VMEM)

    def struct(*shape):
        return jax.ShapeDtypeStruct(shape, jnp.float32)

    mine = (place // per_z) * CORES + core
    part = lookup(lax.dynamic_slice_in_dim(classes, mine * strip, strip, axis=1), table)
    from_below = slab_shift(part, 1)
    from_above = slab_shift(part, -1)
    groups = [
        [z * per_z + y * CORES + c for z in range(depth) for c in range(CORES)] for y in range(Y_LO)
    ]
    halo = lax.all_gather(jnp.stack([from_below, from_above]), "src", axis_index_groups=groups)

    entries = jnp.concatenate([receivers[0].T.astype(jnp.float32), misfit], axis=0)
    below = slab_shift(entries, 1)
    above = slab_shift(entries, -1)
    bottom, top, below, above = lax.optimization_barrier(
        (forward[:1], forward[-1:], below, above)
    )
    lower = slab_shift(top, 1)
    upper = slab_shift(bottom, -1)

    vmem = pl.BlockSpec(memory_space=pltpu.VMEM)
    anywhere = pl.BlockSpec(memory_space=pl.ANY)
    smem = pl.BlockSpec(memory_space=pltpu.SMEM)
    deep = layers + 2 * REACH
    side, own = pl.pallas_call(
        scatter_kernel,
        out_shape=(struct(deep, rows, columns), struct(layers, rows, columns)),
        in_specs=[vmem, vmem, vmem, vmem, smem],
        compiler_params=params,
        name="scatter",
    )(below, entries, above, classes, table)

    tall = rows + 2 * PAD
    thick = layers + 2
    w0, w1, w2, sums = pl.pallas_call(
        vectors_kernel,
        out_shape=(struct(thick, rows, columns),) * 3 + (struct(8, 128),),
        in_specs=[anywhere, anywhere, vmem],
        out_specs=(anywhere, anywhere, anywhere, vmem),
        scratch_shapes=[
            pltpu.VMEM((deep + 2, tall, columns), jnp.float32),
            pltpu.VMEM((deep, rows, columns), jnp.float32),
            pltpu.VMEM((deep, tall, columns), jnp.float32),
            pltpu.VMEM((deep, rows, columns), jnp.float32),
            pltpu.VMEM((deep, rows, columns), jnp.float32),
            pltpu.VMEM((deep, tall, columns), jnp.float32),
            pltpu.VMEM((deep - 2, tall, columns), jnp.float32),
            pltpu.VMEM((deep - 4, tall, columns), jnp.float32),
            pltpu.SemaphoreType.DMA((2 * blocks + 1,)),
        ],
        compiler_params=params,
        name="vectors",
    )(own, halo, side)

    sums = lax.all_to_all(jnp.broadcast_to(sums[None], (count, 8, 128)), "slab", 0, 0)
    half = rows // sources
    adjoint, keep, give = pl.pallas_call(
        terms_kernel,
        out_shape=(struct(layers, rows, columns),) + (struct(blocks, layers * half, columns),) * 2,
        scratch_shapes=[pltpu.VMEM((thick, tall, columns), jnp.float32)] * 2,
        compiler_params=params,
        name="terms",
    )(sums, w0, w1, w2, forward, lower, upper)

    got = lax.ppermute(give, "src", [(i, i ^ 1) for i in range(sources)])
    groups = [
        [z * per_z + y * CORES + c for z in range(depth) for y in range(Y_LO)] for c in range(CORES)
    ]
    shares = lax.all_to_all(keep + got, "src", 0, 0, axis_index_groups=groups)
    gradient = jnp.sum(shares, axis=0).reshape(layers, half, columns)
    return (adjoint[None], gradient)


def solution(mesh):
    placed = (
        P("src", "slab", None, None),
        P("src", "slab"),
        P("src", "slab", None),
        P("slab", None, None),
        P(),
    )
    return jax.shard_map(
        body,
        mesh=mesh,
        in_specs=placed,
        out_specs=(P("src", "slab", None, None), P("slab", "src", None)),
        check_vma=False,
    )
```

time: 286 us -> 176 us (0.62)
  other arithmetic: 124 us -> 4.59 us
  Pallas kernels: 0 us -> 63 us
  local copies, waits for them, and re-layouts: 52 us -> 4.85 us
  between operations: 23.8 us -> 14.2 us
  waiting for transfers between devices: 15.4 us -> 22.9 us
  blocking collectives: 40.1 us -> 35.3 us
    pallas_call x0 -> x3, Pallas kernels: none -> 63 us  [the longest x1 28.4 us: body(): pl.pallas_call(vectors_kernel, out_shape=(struct(thick, rows, columns),)...]
    mul x4 -> x0, other arithmetic: 53.2 us -> none  [the longest x1 18.2 us: body(): second_field = spread0 * inverse[1:-1]]
    slice x17 -> x1, local copies, waits for them, and re-layouts: 28 us -> 1.32 us  [body(): forward[-1:]]
    select_n x3 -> x0, other arithmetic: 26.3 us -> none  [the longest x2 24.8 us: lookup(): result = jnp.where(classes == label, table[label], result)]
    scatter-add x1 -> x0, other arithmetic: 24.3 us -> none  [body(): right_side = jnp.zeros((size,), jnp.float32).at[jnp.where(inside, cells,...]
    reduce_sum x4 -> x2, other arithmetic: 10.3 us -> 1.03 us  [the longest x1 0.96 us: lookup(): jnp.sum(jnp.where(classes[None] == labels, table[:, None, None, None], 0....]
    all_gather x1, waiting for transfers between devices: 0.01 us -> 9.01 us  [body(): lax.all_gather(jnp.stack([from_below, from_above]), 'src', axis_index_gro...]
    unnamed x25 -> x13, local copies, waits for them, and re-layouts: 8.74 us -> 1.29 us
  transfers between devices with their start and end apart: 9 -> 9, of which waited for: 4 -> 5; matrix products, arithmetic and copies ran while one was open for 50% -> 2% of each run, Pallas kernels for 0% -> 28%
where the time goes in v2:
time: 176 us; the launch traced here: 175 us
  Pallas kernels  63 us (36%)
  blocking collectives  35.3 us (20%)
  starting transfers between devices  30.3 us (17%)
  waiting for transfers between devices  22.9 us (13%)
  between operations  14.2 us (8%)
  local copies, waits for them, and re-layouts  4.85 us (3%)
  other arithmetic  4.59 us (3%)
    all_to_all x1, blocking collectives, body(): shares = lax.all_to_all(keep + got, 'src', 0, 0, axis_index_groups=groups)  35.3 us
    pallas_call x1, Pallas kernels, body(): pl.pallas_call(vectors_kernel, out_shape=(struct(thick, rows, columns),)...  28.4 us
    ppermute x6, starting transfers between devices, slab_shift(): return lax.ppermute(value, 'slab', pairs)  22.2 us
    pallas_call x1, Pallas kernels, body(): pl.pallas_call(scatter_kernel, out_shape=(struct(deep, rows, columns), st...  21.4 us
    pallas_call x1, Pallas kernels, body(): pl.pallas_call(terms_kernel, out_shape=(struct(layers, rows, columns),) +...  13.1 us
    all_gather x1, waiting for transfers between devices, body(): lax.all_gather(jnp.stack([from_below, from_above]), 'src', axis_index_gro...  9.01 us
    all_to_all x1, waiting for transfers between devices, body(): lax.all_to_all(jnp.broadcast_to(sums[None], (count, 8, 128)), 'slab', 0, 0)  6.53 us
    all_to_all x1, starting transfers between devices, body(): lax.all_to_all(jnp.broadcast_to(sums[None], (count, 8, 128)), 'slab', 0, 0)  6.41 us
  transfers between devices with their start and end apart: 9, of which 5 were waited for; matrix products, arithmetic and copies ran while one was open for 2% of the time, Pallas kernels for 28%

profile of v2, /device:TPU:1, one launch (start us, length us, event | category | flops | bytes accessed | tf_op | source)
XLA Modules:
  0.0 175.2 jit_solution(15903959611268387851)
XLA Ops:
  7.2 0.0 all-gather.3.cloned.1.call-start
  7.2 0.9 constant_dynamic-slice_fusion
  8.2 1.0 select_reduce_fusion
  9.1 1.3 collective-permute-start.3
  10.4 6.3 %collective-permute-start.2 = (f32[4,24,384]{2,1,0:T(8,128)S(1)}, f32[4,24,384]{2,1,0:T(8,128)S(1)}, u32[]{:S(2)}, u32[]{:S(2)}) collective-permute-start(f32[4,24,384]{2,1,0:T(8,128)S(1)} %select_reduce_fusion), channel_id=1, source_target_pairs={{0,1},{1,2},{2,3},{3,4},{4,5},{5,6},{6,7},{8,9},{9,10},{10,11},{11... | collective-permute-start | bytes 442376 | tf_op jit(solution)/shard_map/ppermute | solution.py:25
  16.7 0.6 collective-permute-done.3
  17.3 4.1 %collective-permute-done.2 = f32[4,24,384]{2,1,0:T(8,128)S(1)} collective-permute-done((f32[4,24,384]{2,1,0:T(8,128)S(1)}, f32[4,24,384]{2,1,0:T(8,128)S(1)}, u32[]{:S(2)}, u32[]{:S(2)}) %collective-permute-start.2) | collective-permute-done | bytes 147488 | tf_op jit(solution)/shard_map/ppermute | solution.py:25
  21.4 0.7 pad_maximum_fusion
  22.1 0.0 all-gather.3.cloned.1.call-update
  22.1 0.7 convert_bitcast_fusion
  22.8 0.7 pad_maximum_fusion.1.own
  23.5 0.0 copy-start.3
  23.5 1.3 collective-permute-start.1
  24.8 6.2 %collective-permute-start = (f32[3,1152]{1,0:T(4,128)S(1)}, f32[3,1152]{1,0:T(4,128)S(1)}, u32[]{:S(2)}, u32[]{:S(2)}) collective-permute-start(f32[3,1152]{1,0:T(4,128)S(1)} %pad_maximum_fusion.1.own), channel_id=1, source_target_pairs={{0,1},{1,2},{2,3},{3,4},{4,5},{5,6},{6,7},{8,9},{9,10},{10,11},{11... | collective-permute-start | bytes 41480 | tf_op jit(solution)/shard_map/ppermute | solution.py:25
  31.1 1.3 slice_bitcast_fusion
  32.4 0.0 collective-permute-done.1.above
  32.4 0.0 copy-start.4
  32.4 0.0 collective-permute-done.below
  32.4 0.0 copy-start.5
  32.5 5.8 %collective-permute-start.4 = (f32[1,384,384]{2,1,0:T(8,128)S(1)}, f32[1,384,384]{2,1,0:T(8,128)S(1)}, u32[]{:S(2)}, u32[]{:S(2)}) collective-permute-start(f32[1,384,384]{2,1,0:T(8,128)S(1)} %get-tuple-element.23), channel_id=1, source_target_pairs={{0,1},{1,2},{2,3},{3,4},{4,5},{5,6},{6,7},{8,9},{9,10},{10,11},{11... | collective-permute-start | bytes 1769480 | tf_op jit(solution)/shard_map/ppermute | solution.py:25
  38.3 1.3 collective-permute-start.5
  39.6 0.0 copy-done.3
  39.6 0.0 copy-done.4
  39.6 0.0 copy-done.5
  39.6 21.4 %scatter.1 = (f32[10,384,384]{2,1,0:T(8,128)}, f32[4,384,384]{2,1,0:T(8,128)}) custom-call(f32[3,1152]{1,0:T(4,128)} %copy-done.5, f32[3,1152]{1,0:T(4,128)} %copy-done.3, f32[3,1152]{1,0:T(4,128)} %copy-done.4, s32[4,384,384]{2,1,0:T(8,128)} %classes.1, f32[16]{0:T(128)} %table.1), custom_call_target="tpu_custom_call" | custom-call | tf_op jit(solution)/shard_map/scatter/pallas_call | solution.py:355
  61.0 9.0 %all-gather.3.cloned.1.call-done = f32[32,4,24,384]{3,2,1,0:T(8,128)} async-done(((f32[2,4,24,384]{3,2,1,0:T(8,128)}), f32[32,4,24,384]{3,2,1,0:T(8,128)}) %all-gather.3.cloned.1.call-update) | async-done | bytes 4718608 | tf_op jit(solution)/shard_map/all_gather | solution.py:340
  70.1 28.4 %vectors.1 = (f32[6,384,384]{2,1,0:T(8,128)}, f32[6,384,384]{2,1,0:T(8,128)}, f32[6,384,384]{2,1,0:T(8,128)}, f32[8,128]{1,0:T(8,128)}) custom-call(f32[4,384,384]{2,1,0:T(8,128)} %get-tuple-element.17.own, f32[16,2,4,24,384]{4,3,2,1,0:T(8,128)} %bitcast.14, f32[10,384,384]{2,1,0:T(8,128)} %get-tuple-element.18.side), custom_call_target="tpu_custom_call" | custom-call | tf_op jit(solution)/shard_map/vectors/pallas_call | solution.py:365
  98.5 1.3 broadcast_in_dim.26
  99.8 6.4 %all-to-all-start = ((f32[8,8,128]{2,1,0:T(8,128)}), f32[8,8,128]{2,1,0:T(8,128)S(1)}, u32[]{:S(2)}, u32[]{:S(2)}) async-start(f32[8,8,128]{2,1,0:T(8,128)} %broadcast_in_dim.26), calls=%async_computation | async-start | bytes 65536 | tf_op jit(solution)/shard_map/all_to_all | solution.py:385
  106.2 0.0 collective-permute-done.4.lower
  106.2 0.0 copy-start
  106.2 0.0 collective-permute-done.5.upper
  106.2 0.0 copy-start.1
  106.2 6.5 %all-to-all-done.sums = f32[8,8,128]{2,1,0:T(8,128)S(1)} async-done(((f32[8,8,128]{2,1,0:T(8,128)}), f32[8,8,128]{2,1,0:T(8,128)S(1)}, u32[]{:S(2)}, u32[]{:S(2)}) %all-to-all-start) | async-done | bytes 32800 | tf_op jit(solution)/shard_map/all_to_all | solution.py:385
  112.7 0.0 copy-start.2
  112.7 0.0 copy-done
  112.7 0.0 copy-done.1
  112.7 0.6 copy-done.2
  113.4 13.1 %terms.1 = (f32[4,384,384]{2,1,0:T(8,128)}, f32[16,48,384]{2,1,0:T(8,128)}, f32[16,48,384]{2,1,0:T(8,128)}) custom-call(f32[8,8,128]{2,1,0:T(8,128)} %copy-done.2, f32[6,384,384]{2,1,0:T(8,128)} %get-tuple-element.20.w0, f32[6,384,384]{2,1,0:T(8,128)} %get-tuple-element.21.w1, f32[6,384,384]{2,1,0:T(8,128)} %get-tuple-element.22.w2, ...), custom_call_target="tpu_custom_call" | custom-call | tf_op jit(solution)/shard_map/terms/pallas_call | solution.py:387
  126.5 1.7 collective-permute-start.6
  128.2 2.7 %collective-permute-done.6 = f32[16,48,384]{2,1,0:T(8,128)S(1)} collective-permute-done((f32[16,48,384]{2,1,0:T(8,128)}, f32[16,48,384]{2,1,0:T(8,128)S(1)}, u32[]{:S(2)}, u32[]{:S(2)}) %collective-permute-start.6) | collective-permute-done | bytes 1179680 | tf_op jit(solution)/shard_map/ppermute | solution.py:395
  130.8 1.4 add.17
  132.3 35.3 %all_to_all.10 = f32[16,48,384]{2,1,0:T(8,128)S(1)} all-to-all(f32[16,48,384]{2,1,0:T(8,128)S(1)} %add.17), channel_id=1, replica_groups={{0,16,32,48,64,80,96,112,128,144,160,176,192,208,224,240},{8,24,40,56,7..., dimensions={0} | all-to-all | bytes 2359296 | tf_op jit(solution)/shard_map/all_to_all | solution.py:399
  167.6 0.1 reduce_sum.19
  167.6 0.7 copy.9
  (1 shorter events, 0.0 us)
Async XLA Ops:
  7.2 62.9 %all-gather.3.cloned.1.call-start = ((), (), s32[]{:S(2)}) async-start(), calls=%async_computation.2 | async-start | bytes 5013504 | tf_op jit(solution)/shard_map/all_gather | solution.py:340
  9.1 8.2 %collective-permute-start.3 = (f32[4,24,384]{2,1,0:T(8,128)S(1)}, f32[4,24,384]{2,1,0:T(8,128)S(1)}, u32[]{:S(2)}, u32[]{:S(2)}) collective-permute-start(f32[4,24,384]{2,1,0:T(8,128)S(1)} %select_reduce_fusion), channel_id=1, source_target_pairs={{1,0},{2,1},{3,2},{4,3},{5,4},{6,5},{7,6},{9,8},{10,9},{11,10},{12... | collective-permute-start | bytes 442376 | tf_op jit(solution)/shard_map/ppermute | solution.py:25
  10.4 10.9 %collective-permute-start.2 = (f32[4,24,384]{2,1,0:T(8,128)S(1)}, f32[4,24,384]{2,1,0:T(8,128)S(1)}, u32[]{:S(2)}, u32[]{:S(2)}) collective-permute-start(f32[4,24,384]{2,1,0:T(8,128)S(1)} %select_reduce_fusion), channel_id=1, source_target_pairs={{0,1},{1,2},{2,3},{3,4},{4,5},{5,6},{6,7},{8,9},{9,10},{10,11},{11... | collective-permute-start | bytes 442376 | tf_op jit(solution)/shard_map/ppermute | solution.py:25
  23.5 16.0 %copy-start.3 = (f32[3,1152]{1,0:T(4,128)}, f32[3,1152]{1,0:T(4,128)S(1)}, u32[]{:S(2)}) copy-start(f32[3,1152]{1,0:T(4,128)S(1)} %pad_maximum_fusion.1.own) | copy-start | bytes 41476
  23.5 8.9 %collective-permute-start.1 = (f32[3,1152]{1,0:T(4,128)S(1)}, f32[3,1152]{1,0:T(4,128)S(1)}, u32[]{:S(2)}, u32[]{:S(2)}) collective-permute-start(f32[3,1152]{1,0:T(4,128)S(1)} %pad_maximum_fusion.1.own), channel_id=1, source_target_pairs={{1,0},{2,1},{3,2},{4,3},{5,4},{6,5},{7,6},{9,8},{10,9},{11,10},{12... | collective-permute-start | bytes 41480 | tf_op jit(solution)/shard_map/ppermute | solution.py:25
  24.8 7.6 %collective-permute-start = (f32[3,1152]{1,0:T(4,128)S(1)}, f32[3,1152]{1,0:T(4,128)S(1)}, u32[]{:S(2)}, u32[]{:S(2)}) collective-permute-start(f32[3,1152]{1,0:T(4,128)S(1)} %pad_maximum_fusion.1.own), channel_id=1, source_target_pairs={{0,1},{1,2},{2,3},{3,4},{4,5},{5,6},{6,7},{8,9},{9,10},{10,11},{11... | collective-permute-start | bytes 41480 | tf_op jit(solution)/shard_map/ppermute | solution.py:25
  32.4 7.2 %copy-start.4 = (f32[3,1152]{1,0:T(4,128)}, f32[3,1152]{1,0:T(4,128)S(1)}, u32[]{:S(2)}) copy-start(f32[3,1152]{1,0:T(4,128)S(1)} %collective-permute-done.1.above) | copy-start | bytes 41476
  32.4 7.1 %copy-start.5 = (f32[3,1152]{1,0:T(4,128)}, f32[3,1152]{1,0:T(4,128)S(1)}, u32[]{:S(2)}) copy-start(f32[3,1152]{1,0:T(4,128)S(1)} %collective-permute-done.below) | copy-start | bytes 41476
  32.5 73.7 %collective-permute-start.4 = (f32[1,384,384]{2,1,0:T(8,128)S(1)}, f32[1,384,384]{2,1,0:T(8,128)S(1)}, u32[]{:S(2)}, u32[]{:S(2)}) collective-permute-start(f32[1,384,384]{2,1,0:T(8,128)S(1)} %get-tuple-element.23), channel_id=1, source_target_pairs={{0,1},{1,2},{2,3},{3,4},{4,5},{5,6},{6,7},{8,9},{9,10},{10,11},{11... | collective-permute-start | bytes 1769480 | tf_op jit(solution)/shard_map/ppermute | solution.py:25
  38.3 67.9 %collective-permute-start.5 = (f32[1,384,384]{2,1,0:T(8,128)S(1)}, f32[1,384,384]{2,1,0:T(8,128)S(1)}, u32[]{:S(2)}, u32[]{:S(2)}) collective-permute-start(f32[1,384,384]{2,1,0:T(8,128)S(1)} %get-tuple-element.24), channel_id=1, source_target_pairs={{1,0},{2,1},{3,2},{4,3},{5,4},{6,5},{7,6},{9,8},{10,9},{11,10},{12... | collective-permute-start | bytes 1769480 | tf_op jit(solution)/shard_map/ppermute | solution.py:25
  99.8 13.0 %all-to-all-start = ((f32[8,8,128]{2,1,0:T(8,128)}), f32[8,8,128]{2,1,0:T(8,128)S(1)}, u32[]{:S(2)}, u32[]{:S(2)}) async-start(f32[8,8,128]{2,1,0:T(8,128)} %broadcast_in_dim.26), calls=%async_computation | async-start | bytes 65536 | tf_op jit(solution)/shard_map/all_to_all | solution.py:385
  106.2 6.6 %copy-start = (f32[1,384,384]{2,1,0:T(8,128)}, f32[1,384,384]{2,1,0:T(8,128)S(1)}, u32[]{:S(2)}) copy-start(f32[1,384,384]{2,1,0:T(8,128)S(1)} %collective-permute-done.4.lower) | copy-start | bytes 1769476
  106.2 6.6 %copy-start.1 = (f32[1,384,384]{2,1,0:T(8,128)}, f32[1,384,384]{2,1,0:T(8,128)S(1)}, u32[]{:S(2)}) copy-start(f32[1,384,384]{2,1,0:T(8,128)S(1)} %collective-permute-done.5.upper) | copy-start | bytes 1769476
  112.7 0.6 copy-start.2
  126.5 4.4 %collective-permute-start.6 = (f32[16,48,384]{2,1,0:T(8,128)}, f32[16,48,384]{2,1,0:T(8,128)S(1)}, u32[]{:S(2)}, u32[]{:S(2)}) collective-permute-start(f32[16,48,384]{2,1,0:T(8,128)} %get-tuple-element.27), channel_id=1, source_target_pairs={{0,8},{8,0},{16,24},{24,16},{32,40},{40,32},{48,56},{56,48},{64,72... | collective-permute-start | bytes 3538952 | tf_op jit(solution)/shard_map/ppermute | solution.py:395
Sparse Core Ops, SparseCore 0:
  22.2 47.7 all-gather.2

commit v3 on v2

--- a/solution.py
+++ b/solution.py
@@ -9,9 +9,12 @@
 Y_LO = 2
 REACH = 3
 PAD = 8
-ROWS = 96
-GROUP = 4
-VMEM = 56 * 1024 * 1024
+ROWS = 16
+UNROLL = 24
+GROUP = 2
+PARTS = 8
+PIECES = 3
+MIB = 1024 * 1024
 
 
 def lookup(classes, table):
@@ -19,17 +22,16 @@
     return jnp.sum(jnp.where(classes[None] == labels, table[:, None, None, None], 0.0), axis=0)
 
 
-def slab_shift(value, step):
+def slab_ring(value, step):
     count = lax.axis_size("slab")
-    pairs = [(i, i + step) for i in range(count) if 0 <= i + step < count]
-    return lax.ppermute(value, "slab", pairs)
+    return lax.ppermute(value, "slab", [(i, (i + step) % count) for i in range(count)])
 
 
 def scatter_kernel(below, own, above, classes, table, side, conduct):
     layers, rows, columns = classes.shape
     slab = lax.axis_index("slab")
-    count = own.shape[1]
-    across = lax.broadcasted_iota(jnp.int32, (columns, count), 0)
+    count = own.shape[1] * PIECES
+    across = lax.broadcasted_iota(jnp.int32, (count, columns), 1)
     down = lax.broadcasted_iota(jnp.int32, (rows, count), 0)
     sources = (
         (below, range(layers - REACH, layers), 0),
@@ -37,27 +39,31 @@
         (above, range(REACH), REACH + layers),
     )
     for number, (entries, planes, start) in enumerate(sources):
-        first = entries[0:1, :] - ((slab + number - 1) * layers).astype(jnp.float32)
-        index = entries[1:2, :]
-        value = entries[2:3, :]
+        top = entries.shape[0] - 3 * PIECES
+        lines = [entries[row : row + 1, :] for row in range(top, entries.shape[0])]
+        first, index, value = [
+            jnp.concatenate(lines[at * PIECES : (at + 1) * PIECES], axis=1) for at in range(3)
+        ]
+        first = first - ((slab + number - 1) * layers).astype(jnp.float32)
         line = jnp.floor((index + 0.5) * (1.0 / columns))
-        column = (index - line * columns).astype(jnp.int32)
         place = (first * rows + line).astype(jnp.int32)
-        hit = across == column
+        upright = jnp.transpose(
+            jnp.concatenate([index - line * columns, value] + [value * 0.0] * 6, axis=0)
+        )
+        hit = across == upright[:, 0:1].astype(jnp.int32)
         parts = []
-        rest = value
+        rest = upright[:, 1:2]
         for _ in range(3):
-            piece = rest.astype(jnp.bfloat16)
-            rest = rest - piece.astype(jnp.float32)
-            parts.append(jnp.where(hit, piece.astype(jnp.float32), 0.0).astype(jnp.bfloat16))
+            piece = rest.astype(jnp.bfloat16).astype(jnp.float32)
+            rest = rest - piece
+            parts.append(jnp.where(hit, piece, 0.0).astype(jnp.bfloat16))
+        parts = jnp.concatenate(parts, axis=1)
         for step, plane in enumerate(planes):
             chosen = jnp.where(down + plane * rows == place, 1.0, 0.0).astype(jnp.bfloat16)
-            total = 0.0
-            for part in parts:
-                total = total + lax.dot_general(
-                    chosen, part, (((1,), (1,)), ((), ())), preferred_element_type=jnp.float32
-                )
-            side[start + step] = total
+            total = jnp.dot(chosen, parts, preferred_element_type=jnp.float32)
+            side[start + step] = (
+                total[:, :columns] + total[:, columns : 2 * columns] + total[:, 2 * columns :]
+            )
 
     values = [table[label] for label in range(table.shape[0])]
 
@@ -67,7 +73,7 @@
             conduct[layer, pl.ds(at, ROWS), :] = choose(classes[layer, pl.ds(at, ROWS), :], values)
         return carry
 
-    lax.fori_loop(0, rows // ROWS, strip, 0)
+    sweep(rows // ROWS, strip, 0)
 
 
 def choose(labels, values):
@@ -79,21 +85,43 @@
     return values[0]
 
 
-def vectors_kernel(own, halo, side, out0, out1, out2, sums, cond, near_x, near_y, near_z, inverse, f0, f1, f2, marks):
+def sweep(count, step, carry, unroll=None):
+    unroll = unroll or UNROLL
+
+    def several(at, inner):
+        for number in range(unroll):
+            inner = step(at * unroll + number, inner)
+        return inner
+
+    return lax.fori_loop(0, count // unroll, several, carry)
+
+
+def reciprocal(value):
+    guess = pl.reciprocal(value, approx=True)
+    for _ in range(2):
+        guess = guess * (2.0 - value * guess)
+    return guess
+
+
+def vectors_kernel(
+    own, halo, side, f0, f1, f2, sums, cond, near_x, near_y, near_z, inverse, marks
+):
     layers, rows, columns = own.shape
     blocks, _, _, strip, _ = halo.shape
     filled = pl.ds(PAD, rows)
-    copies = [
-        pltpu.make_async_copy(own, cond.at[pl.ds(layers, layers), filled], marks.at[0])
-    ]
+    first_copies, copies = [], []
+
+    def fetch(source, target, group):
+        mark = marks.at[len(first_copies) + len(copies)]
+        copy = pltpu.make_async_copy(source, target, mark)
+        copy.start()
+        group.append(copy)
+
+    fetch(own, cond.at[pl.ds(layers, layers), filled], first_copies)
     for block in range(blocks):
         for step in range(2):
             target = cond.at[pl.ds(2 * step * layers, layers), pl.ds(PAD + block * strip, strip)]
-            copies.append(
-                pltpu.make_async_copy(halo.at[block, step], target, marks.at[len(copies)])
-            )
-    for copy in copies:
-        copy.start()
+            fetch(halo.at[block, step], target, copies)
     slab = lax.axis_index("slab")
     slabs = lax.axis_size("slab")
     deep = layers + 2 * REACH
@@ -103,8 +131,6 @@
         for plane in range(ref.shape[0]):
             ref[plane, 0:PAD, :] = blank
             ref[plane, PAD + rows : 2 * PAD + rows, :] = blank
-    for copy in copies:
-        copy.wait()
 
     def here(at):
         return pl.ds(pl.multiple_of(at * ROWS + PAD, PAD), ROWS)
@@ -134,20 +160,23 @@
             right = jnp.where(lane == columns - 1, 0.0, pltpu.roll(centre, columns - 1, 1))
             left = jnp.where(lane == 0, 0.0, pltpu.roll(centre, 1, 1))
             total = 6.0 * centre + ((lower + upper) + (ahead + behind) + (left + right))
-            turned = (2.0 * scale) / (total + (1.0 - scale))
+            turned = scale * reciprocal(total + (1.0 - scale))
             inverse[plane, plain(at), :] = turned
-            near_x[plane, plain(at), :] = jnp.where(lane == columns - 1, 0.0, 0.5 * (centre + right))
-            near_y[plane, here(at), :] = 0.5 * (centre + ahead)
-            near_z[plane, plain(at), :] = 0.5 * (centre + upper)
-            f0[plane, here(at), :] = side[plane, plain(at), :] * turned
+            near_x[plane, plain(at), :] = jnp.where(lane == columns - 1, 0.0, centre + right)
+            near_y[plane, here(at), :] = centre + ahead
+            near_z[plane, plain(at), :] = centre + upper
+            f0[plane, here(at), :] = side[plane, plain(at), :] * (2.0 * turned)
             return inner
 
-        return lax.fori_loop(0, strips, step, carry)
-
-    lax.fori_loop(0, deep, setup, 0)
-    thick = layers + 2
-    write0 = pltpu.make_async_copy(f0.at[pl.ds(2, thick), filled], out0, marks.at[0])
-    write0.start()
+        return sweep(strips, step, carry)
+
+    for copy in first_copies:
+        copy.wait()
+    lax.fori_loop(REACH + 1, REACH + layers - 1, setup, 0)
+    for copy in copies:
+        copy.wait()
+    lax.fori_loop(0, REACH + 1, setup, 0)
+    lax.fori_loop(REACH + layers - 1, deep, setup, 0)
 
     def spread(field, offset, plane, at):
         centre = field[plane, here(at), :]
@@ -175,7 +204,7 @@
                 target[plane - 1, here(at), :] = total * inverse[plane + offset, plain(at), :]
                 return inner
 
-            lax.fori_loop(0, strips, step, 0)
+            sweep(strips, step, 0)
 
     zero = jnp.zeros((8, columns), jnp.float32)
 
@@ -191,7 +220,7 @@
                 s2 + fold(value * total),
             )
 
-        return lax.fori_loop(0, strips, step, carry)
+        return sweep(strips, step, carry)
 
     def inside1(plane, carry):
         def step(at, inner):
@@ -201,30 +230,26 @@
             f2[plane - 1, here(at), :] = value
             return s3 + fold(centre * total), s4 + fold(value * total)
 
-        return lax.fori_loop(0, strips, step, carry)
+        return sweep(strips, step, carry)
 
     def inside2(plane, carry):
         def step(at, inner):
             centre, total = spread(f2, 2, plane, at)
             return inner + fold(centre * total)
 
-        return lax.fori_loop(0, strips, step, carry)
+        return sweep(strips, step, carry)
 
     outer(f0, 0, f1, (1, 2, deep - 3, deep - 2))
     s0, s1, s2 = lax.fori_loop(REACH, REACH + layers, inside0, (zero, zero, zero))
-    write1 = pltpu.make_async_copy(f1.at[pl.ds(1, thick), filled], out1, marks.at[1])
-    write1.start()
     outer(f1, 1, f2, (1, deep - 4))
     s3, s4 = lax.fori_loop(REACH - 1, REACH - 1 + layers, inside1, (zero, zero))
-    write2 = pltpu.make_async_copy(f2.at[:, filled], out2, marks.at[2])
-    write2.start()
     s5 = lax.fori_loop(REACH - 2, REACH - 2 + layers, inside2, zero)
-    for row, total in enumerate((s0, s1, s2, s3, s4, s5)):
+    for row, total in enumerate((2.0 * s0, s1, s2, s3, s4, s5)):
         single = jnp.sum(jnp.sum(total, axis=0, keepdims=True), axis=1, keepdims=True)
-        sums[row : row + 1, :] = jnp.broadcast_to(single, (1, sums.shape[1]))
-    sums[6:8, :] = jnp.zeros((2, sums.shape[1]), jnp.float32)
-    for copy in (write0, write1, write2):
-        copy.wait()
+        for target in range(sums.shape[0]):
+            sums[target, row : row + 1, :] = jnp.broadcast_to(single, (1, sums.shape[2]))
+    for target in range(sums.shape[0]):
+        sums[target, 6:8, :] = jnp.zeros((2, sums.shape[2]), jnp.float32)
 
 
 def weights(moments):
@@ -245,38 +270,61 @@
     return c0, c1, c2
 
 
-def terms_kernel(sums, w0, w1, w2, forward, lower, upper, adjoint, keep, give, adj, fwd):
+def terms_kernel(
+    sums, w0, w1, w2, forward, lower, upper, adjoint, keep, give, adj, fwd, marks
+):
     layers, rows, columns = forward.shape
     pairs, _, _ = keep.shape
     strip = rows // pairs
     half = strip // 2
+    thick = layers + 2
     first = lax.axis_index("src") % CORES == 0
+    slab = lax.axis_index("slab")
+    filled = pl.ds(PAD, rows)
+    fields = []
+    for number, (source, start, count) in enumerate(
+        ((lower, 0, 1), (forward, 1, layers), (upper, layers + 1, 1))
+    ):
+        target = fwd.at[pl.ds(start, count), filled]
+        fields.append(pltpu.make_async_copy(source, target, marks.at[number]))
+        fields[-1].start()
     blank = jnp.zeros((PAD, columns), jnp.float32)
     for ref in (adj, fwd):
-        for plane in range(layers + 2):
+        for plane in range(thick):
             ref[plane, 0:PAD, :] = blank
             ref[plane, PAD + rows : 2 * PAD + rows, :] = blank
-    fwd[0, PAD : PAD + rows, :] = lower[0]
-    fwd[layers + 1, PAD : PAD + rows, :] = upper[0]
     total = sums[0]
     for other in range(1, sums.shape[0]):
         total = total + sums[other]
     c0, c1, c2 = weights([total[i : i + 1, 0:1] for i in range(6)])
     c0, c1, c2 = [jnp.broadcast_to(c, (ROWS, columns)) for c in (c0, c1, c2)]
 
-    for plane in range(layers + 2):
-
+    written = []
+    for plane in range(thick):
         def mix(at, carry, plane=plane):
-            span = pl.ds(pl.multiple_of(at * ROWS, ROWS), ROWS)
             wide = pl.ds(pl.multiple_of(at * ROWS + PAD, PAD), ROWS)
-            value = c0 * w0[plane, span, :] + c1 * w1[plane, span, :] + c2 * w2[plane, span, :]
-            adj[plane, wide, :] = value
-            if 0 < plane <= layers:
-                adjoint[plane - 1, span, :] = value
-                fwd[plane, wide, :] = forward[plane - 1, span, :]
+            adj[plane, wide, :] = (
+                c0 * w0[plane + 2, wide, :] + c1 * w1[plane + 1, wide, :] + c2 * w2[plane, wide, :]
+            )
             return carry
 
-        lax.fori_loop(0, rows // ROWS, mix, 0)
+        sweep(rows // ROWS, mix, 0)
+        if 0 < plane <= layers:
+            mark = marks.at[3 + len(written)]
+            written.append(
+                pltpu.make_async_copy(adj.at[plane, filled], adjoint.at[plane - 1], mark)
+            )
+            written[-1].start()
+    for copy in fields:
+        copy.wait()
+
+    @pl.when(slab == 0)
+    def _():
+        fwd[0, PAD : PAD + rows, :] = jnp.zeros((rows, columns), jnp.float32)
+
+    @pl.when(slab == lax.axis_size("slab") - 1)
+    def _():
+        fwd[layers + 1, PAD : PAD + rows, :] = jnp.zeros((rows, columns), jnp.float32)
 
     tall = strip * GROUP
     lane = lax.broadcasted_iota(jnp.int32, (tall, columns), 1)
@@ -311,7 +359,9 @@
                 give[block, layer * half : (layer + 1) * half, :] = jnp.where(first, bottom, top)
             return carry
 
-        lax.fori_loop(0, pairs // GROUP, step, 0)
+        sweep(pairs // GROUP, step, 0, PARTS)
+    for copy in written:
+        copy.wait()
 
 
 def body(forward_field, misfit, receivers, classes, table):
@@ -321,32 +371,48 @@
     per_z = CORES * Y_LO
     depth = sources // per_z
     place = lax.axis_index("src")
+    slab = lax.axis_index("slab")
     core = place % CORES
     blocks = depth * CORES
     strip = rows // blocks
     forward = forward_field[0]
-    params = pltpu.CompilerParams(vmem_limit_bytes=VMEM)
 
     def struct(*shape):
         return jax.ShapeDtypeStruct(shape, jnp.float32)
 
+    def kept(*shape):
+        return pltpu.VMEM(shape, jnp.float32)
+
+    def stay(value):
+        return pltpu.with_memory_space_constraint(value, pltpu.VMEM)
+
+    def limit(size):
+        return pltpu.CompilerParams(vmem_limit_bytes=size * MIB)
+
     mine = (place // per_z) * CORES + core
     part = lookup(lax.dynamic_slice_in_dim(classes, mine * strip, strip, axis=1), table)
-    from_below = slab_shift(part, 1)
-    from_above = slab_shift(part, -1)
+    lists = jnp.concatenate([receivers[0].T.astype(jnp.float32), misfit], axis=0)
+    packed = jnp.concatenate(
+        [part.reshape(layers * strip, columns), lists.reshape(3 * PIECES, columns)], axis=0
+    )
+    below = slab_ring(packed, 1)
+    above = slab_ring(packed, -1)
+    shares = jnp.stack(
+        [
+            jnp.where(slab > 0, below[: layers * strip], 0.0),
+            jnp.where(slab < count - 1, above[: layers * strip], 0.0),
+        ]
+    ).reshape(2, layers, strip, columns)
     groups = [
         [z * per_z + y * CORES + c for z in range(depth) for c in range(CORES)] for y in range(Y_LO)
     ]
-    halo = lax.all_gather(jnp.stack([from_below, from_above]), "src", axis_index_groups=groups)
-
-    entries = jnp.concatenate([receivers[0].T.astype(jnp.float32), misfit], axis=0)
-    below = slab_shift(entries, 1)
-    above = slab_shift(entries, -1)
+    halo = lax.all_gather(shares, "src", axis_index_groups=groups)
+
     bottom, top, below, above = lax.optimization_barrier(
         (forward[:1], forward[-1:], below, above)
     )
-    lower = slab_shift(top, 1)
-    upper = slab_shift(bottom, -1)
+    lower = slab_ring(top, 1)
+    upper = slab_ring(bottom, -1)
 
     vmem = pl.BlockSpec(memory_space=pltpu.VMEM)
     anywhere = pl.BlockSpec(memory_space=pl.ANY)
@@ -354,43 +420,51 @@
     deep = layers + 2 * REACH
     side, own = pl.pallas_call(
         scatter_kernel,
-        out_shape=(struct(deep, rows, columns), struct(layers, rows, columns)),
+        out_shape=(kept(deep, rows, columns), kept(layers, rows, columns)),
         in_specs=[vmem, vmem, vmem, vmem, smem],
-        compiler_params=params,
+        compiler_params=limit(24),
         name="scatter",
-    )(below, entries, above, classes, table)
+    )(below, packed, above, classes, table)
 
     tall = rows + 2 * PAD
     thick = layers + 2
     w0, w1, w2, sums = pl.pallas_call(
         vectors_kernel,
-        out_shape=(struct(thick, rows, columns),) * 3 + (struct(8, 128),),
-        in_specs=[anywhere, anywhere, vmem],
-        out_specs=(anywhere, anywhere, anywhere, vmem),
+        out_shape=(
+            kept(deep, tall, columns),
+            kept(deep - 2, tall, columns),
+            kept(deep - 4, tall, columns),
+            struct(count, 8, 128),
+        ),
+        in_specs=[vmem, anywhere, vmem],
+        out_specs=(vmem, vmem, vmem, vmem),
         scratch_shapes=[
             pltpu.VMEM((deep + 2, tall, columns), jnp.float32),
             pltpu.VMEM((deep, rows, columns), jnp.float32),
             pltpu.VMEM((deep, tall, columns), jnp.float32),
             pltpu.VMEM((deep, rows, columns), jnp.float32),
             pltpu.VMEM((deep, rows, columns), jnp.float32),
-            pltpu.VMEM((deep, tall, columns), jnp.float32),
-            pltpu.VMEM((deep - 2, tall, columns), jnp.float32),
-            pltpu.VMEM((deep - 4, tall, columns), jnp.float32),
             pltpu.SemaphoreType.DMA((2 * blocks + 1,)),
         ],
-        compiler_params=params,
+        compiler_params=limit(34),
         name="vectors",
-    )(own, halo, side)
-
-    sums = lax.all_to_all(jnp.broadcast_to(sums[None], (count, 8, 128)), "slab", 0, 0)
+    )(stay(own), halo, stay(side))
+
+    sums = lax.all_to_all(sums, "slab", 0, 0)
     half = rows // sources
     adjoint, keep, give = pl.pallas_call(
         terms_kernel,
         out_shape=(struct(layers, rows, columns),) + (struct(blocks, layers * half, columns),) * 2,
-        scratch_shapes=[pltpu.VMEM((thick, tall, columns), jnp.float32)] * 2,
-        compiler_params=params,
+        in_specs=[vmem] * 4 + [anywhere] * 3,
+        out_specs=(anywhere, vmem, vmem),
+        scratch_shapes=[
+            pltpu.VMEM((thick, tall, columns), jnp.float32),
+            pltpu.VMEM((thick, tall, columns), jnp.float32),
+            pltpu.SemaphoreType.DMA((3 + layers,)),
+        ],
+        compiler_params=limit(16),
         name="terms",
-    )(sums, w0, w1, w2, forward, lower, upper)
+    )(sums, stay(w0), stay(w1), stay(w2), forward, lower, upper)
 
     got = lax.ppermute(give, "src", [(i, i ^ 1) for i in range(sources)])
     groups = [

time: 176 us -> 173 us (0.983)
  Pallas kernels: 63 us -> 40.3 us
  local copies, waits for them, and re-layouts: 4.85 us -> 25 us
  waiting for transfers between devices: 22.9 us -> 35.6 us
  starting transfers between devices: 30.3 us -> 19.3 us
    unnamed x13 -> x27, local copies, waits for them, and re-layouts: 1.29 us -> 22.9 us
    pallas_call x2, Pallas kernels: 49.8 us -> 34.6 us  [the longest x1 18.1 us: body(): pl.pallas_call(vectors_kernel, out_shape=(kept(deep, tall, columns), kept...]
    ppermute x6 -> x4, starting transfers between devices: 22.2 us -> 11.1 us  [slab_ring(): lax.ppermute(value, 'slab', [(i, (i + step) % count) for i in range(count)])]
    all_gather x1, waiting for transfers between devices: 9.01 us -> 18 us  [body(): halo = lax.all_gather(shares, 'src', axis_index_groups=groups)]
    pallas_call x1, Pallas kernels: 13.1 us -> 5.69 us  [body(): pl.pallas_call(terms_kernel, out_shape=(struct(layers, rows, columns),) +...]
    ppermute x6 -> x4, waiting for transfers between devices: 4.65 us -> 8.52 us  [slab_ring(): lax.ppermute(value, 'slab', [(i, (i + step) % count) for i in range(count)])]
  transfers between devices with their start and end apart: 9 -> 7, of which waited for: 5 -> 5; matrix products, arithmetic and copies ran while one was open for 2% -> 1% of each run, Pallas kernels for 28% -> 20%
where the time goes in v3:
time: 173 us
  Pallas kernels  40.3 us (23%)
  waiting for transfers between devices  35.6 us (21%)
  blocking collectives  35 us (20%)
  local copies, waits for them, and re-layouts  25 us (14%)
  starting transfers between devices  19.3 us (11%)
  between operations  14.2 us (8%)
  other arithmetic  3.52 us (2%)
    all_to_all x1, blocking collectives, body(): shares = lax.all_to_all(keep + got, 'src', 0, 0, axis_index_groups=groups)  35 us
    unnamed x27, local copies, waits for them, and re-layouts  22.9 us
    pallas_call x1, Pallas kernels, body(): pl.pallas_call(vectors_kernel, out_shape=(kept(deep, tall, columns), kept...  18.1 us
    all_gather x1, waiting for transfers between devices, body(): halo = lax.all_gather(shares, 'src', axis_index_groups=groups)  18 us
    pallas_call x1, Pallas kernels, body(): pl.pallas_call(scatter_kernel, out_shape=(kept(deep, rows, columns), kept...  16.5 us
    ppermute x4, starting transfers between devices, slab_ring(): lax.ppermute(value, 'slab', [(i, (i + step) % count) for i in range(count)])  11.1 us
    ppermute x4, waiting for transfers between devices, slab_ring(): lax.ppermute(value, 'slab', [(i, (i + step) % count) for i in range(count)])  8.52 us
    all_to_all x1, waiting for transfers between devices, body(): sums = lax.all_to_all(sums, 'slab', 0, 0)  6.55 us
  transfers between devices with their start and end apart: 7, of which 5 were waited for; matrix products, arithmetic and copies ran while one was open for 1% of the time, Pallas kernels for 20%

profile of v3, /device:TPU:1, one launch (start us, length us, event | category | flops | bytes accessed | tf_op | source)
XLA Modules:
  0.0 172.9 jit_solution(6031691542875421396)
XLA Ops:
  7.2 0.0 copy-start.4
  7.2 0.0 all-gather.2.cloned.1.call-start
  7.2 0.9 convert_bitcast_fusion
  8.1 0.7 pad_maximum_fusion.2
  8.8 0.0 copy-start.12
  8.8 0.9 constant_dynamic-slice_fusion
  9.8 1.0 select_reduce_fusion
  10.8 6.0 %collective-permute-start.1 = (f32[105,384]{1,0:T(8,128)S(1)}, f32[105,384]{1,0:T(8,128)S(1)}, u32[]{:S(2)}, u32[]{:S(2)}) collective-permute-start(f32[105,384]{1,0:T(8,128)S(1)} %pad_maximum_fusion.1.own), channel_id=1, source_target_pairs={{0,7},{1,0},{2,1},{3,2},{4,3},{5,4},{6,5},{7,6},{8,15},{9,8},{10,9... | collective-permute-start | bytes 483848 | tf_op jit(solution)/shard_map/ppermute | solution.py:27
  16.8 0.0 collective-permute-start
  16.8 3.1 %collective-permute-done.1.above = f32[105,384]{1,0:T(8,128)S(1)} collective-permute-done((f32[105,384]{1,0:T(8,128)S(1)}, f32[105,384]{1,0:T(8,128)S(1)}, u32[]{:S(2)}, u32[]{:S(2)}) %collective-permute-start.1) | collective-permute-done | bytes 161312 | tf_op jit(solution)/shard_map/ppermute | solution.py:27
  19.9 5.4 %collective-permute-done.below = f32[105,384]{1,0:T(8,128)S(1)} collective-permute-done((f32[105,384]{1,0:T(8,128)S(1)}, f32[105,384]{1,0:T(8,128)S(1)}, u32[]{:S(2)}, u32[]{:S(2)}) %collective-permute-start) | collective-permute-done | bytes 161312 | tf_op jit(solution)/shard_map/ppermute | solution.py:27
  25.3 0.7 pad_maximum_fusion
  26.1 0.0 all-gather.2.cloned.1.call-update
  26.1 0.0 copy-done.4
  26.1 0.0 copy-start.9
  26.1 1.1 slice_bitcast_fusion
  27.2 1.7 collective-permute-start.2
  28.9 3.4 %collective-permute-start.3 = (f32[1,384,384]{2,1,0:T(8,128)}, f32[1,384,384]{2,1,0:T(8,128)}, u32[]{:S(2)}, u32[]{:S(2)}) collective-permute-start(f32[1,384,384]{2,1,0:T(8,128)} %get-tuple-element.24), channel_id=1, source_target_pairs={{0,7},{1,0},{2,1},{3,2},{4,3},{5,4},{6,5},{7,6},{8,15},{9,8},{10,9... | collective-permute-start | bytes 1769480 | tf_op jit(solution)/shard_map/ppermute | solution.py:27
  32.3 0.0 copy-done.12
  32.3 0.0 copy-done.9
  32.3 16.5 %scatter.1 = (f32[10,384,384]{2,1,0:T(8,128)S(1)}, f32[4,384,384]{2,1,0:T(8,128)S(1)}) custom-call(f32[105,384]{1,0:T(8,128)S(1)} %collective-permute-done.below, f32[105,384]{1,0:T(8,128)S(1)} %pad_maximum_fusion.1.own, f32[105,384]{1,0:T(8,128)S(1)} %collective-permute-done.1.above, s32[4,384,384]{2,1,0:T(8,128)S(1)} %copy-done.9, f32[16]{0:T(128)S(1)} %copy-done.12), custom_call_target="tpu_custom_call" | custom-call | tf_op jit(solution)/shard_map/scatter/pallas_call | solution.py:421
  48.8 0.0 copy-start.2
  48.8 2.5 %copy-done.2 = f32[10,384,384]{2,1,0:T(8,128)} copy-done((f32[10,384,384]{2,1,0:T(8,128)}, f32[10,384,384]{2,1,0:T(8,128)S(1)}, u32[]{:S(2)}) %copy-start.2) | copy-done | bytes 5898264
  51.3 0.0 copy-start.10
  51.3 1.4 copy-done.10
  52.7 18.0 %all-gather.2.cloned.1.call-done.halo = f32[16,2,4,24,384]{4,3,2,1,0:T(8,128)} async-done(((f32[1,2,4,24,384]{4,3,2,1,0:T(8,128)}), f32[16,2,4,24,384]{4,3,2,1,0:T(8,128)}) %all-gather.2.cloned.1.call-update) | async-done | bytes 4718608 | tf_op jit(solution)/shard_map/all_gather | solution.py:409
  70.8 0.0 copy-start.3
  70.8 2.7 %copy-done.3 = f32[10,384,384]{2,1,0:T(8,128)S(1)} copy-done((f32[10,384,384]{2,1,0:T(8,128)S(1)}, f32[10,384,384]{2,1,0:T(8,128)}, u32[]{:S(2)}) %copy-start.3) | copy-done | bytes 5898264
  73.4 0.0 copy-start.11
  73.4 1.7 copy-done.11
  75.1 18.1 %vectors.1 = (f32[10,400,384]{2,1,0:T(8,128)S(1)}, f32[8,400,384]{2,1,0:T(8,128)S(1)}, f32[6,400,384]{2,1,0:T(8,128)S(1)}, f32[8,8,128]{2,1,0:T(8,128)}) custom-call(f32[4,384,384]{2,1,0:T(8,128)S(1)} %copy-done.11, f32[16,2,4,24,384]{4,3,2,1,0:T(8,128)} %all-gather.2.cloned.1.call-done.halo, f32[10,384,384]{2,1,0:T(8,128)S(1)} %copy-done.3), custom_call_target="tpu_custom_call" | custom-call | tf_op jit(solution)/shard_map/vectors/pallas_call | solution.py:431
  93.3 0.0 copy-start
  93.3 2.6 %copy-done = f32[10,400,384]{2,1,0:T(8,128)} copy-done((f32[10,400,384]{2,1,0:T(8,128)}, f32[10,400,384]{2,1,0:T(8,128)S(1)}, u32[]{:S(2)}) %copy-start) | copy-done | bytes 6144024
  95.9 0.0 copy-start.5
  95.9 2.3 %copy-done.5 = f32[8,400,384]{2,1,0:T(8,128)} copy-done((f32[8,400,384]{2,1,0:T(8,128)}, f32[8,400,384]{2,1,0:T(8,128)S(1)}, u32[]{:S(2)}) %copy-start.5) | copy-done | bytes 4915224
  98.2 0.0 copy-start.7
  98.2 1.9 %copy-done.7 = f32[6,400,384]{2,1,0:T(8,128)} copy-done((f32[6,400,384]{2,1,0:T(8,128)}, f32[6,400,384]{2,1,0:T(8,128)S(1)}, u32[]{:S(2)}) %copy-start.7) | copy-done | bytes 3686424
  100.1 6.4 %all-to-all-start = ((f32[8,8,128]{2,1,0:T(8,128)}), f32[8,8,128]{2,1,0:T(8,128)S(1)}, u32[]{:S(2)}, u32[]{:S(2)}) async-start(f32[8,8,128]{2,1,0:T(8,128)} %get-tuple-element.19), calls=%async_computation | async-start | bytes 65536 | tf_op jit(solution)/shard_map/all_to_all | solution.py:453
  106.5 0.0 collective-permute-done.2.lower
  106.5 0.0 collective-permute-done.3.upper
  106.5 6.6 %all-to-all-done.sums = f32[8,8,128]{2,1,0:T(8,128)S(1)} async-done(((f32[8,8,128]{2,1,0:T(8,128)}), f32[8,8,128]{2,1,0:T(8,128)S(1)}, u32[]{:S(2)}, u32[]{:S(2)}) %all-to-all-start) | async-done | bytes 32800 | tf_op jit(solution)/shard_map/all_to_all | solution.py:453
  113.1 0.0 copy-start.1
  113.1 2.7 %copy-done.1 = f32[10,400,384]{2,1,0:T(8,128)S(1)} copy-done((f32[10,400,384]{2,1,0:T(8,128)S(1)}, f32[10,400,384]{2,1,0:T(8,128)}, u32[]{:S(2)}) %copy-start.1) | copy-done | bytes 6144024
  115.8 0.0 copy-start.6
  115.8 2.4 %copy-done.6 = f32[8,400,384]{2,1,0:T(8,128)S(1)} copy-done((f32[8,400,384]{2,1,0:T(8,128)S(1)}, f32[8,400,384]{2,1,0:T(8,128)}, u32[]{:S(2)}) %copy-start.6) | copy-done | bytes 4915224
  118.2 0.0 copy-start.8
  118.2 2.0 %copy-done.8 = f32[6,400,384]{2,1,0:T(8,128)S(1)} copy-done((f32[6,400,384]{2,1,0:T(8,128)S(1)}, f32[6,400,384]{2,1,0:T(8,128)}, u32[]{:S(2)}) %copy-start.8) | copy-done | bytes 3686424
  120.3 5.7 %terms.1 = (f32[4,384,384]{2,1,0:T(8,128)}, f32[16,48,384]{2,1,0:T(8,128)S(1)}, f32[16,48,384]{2,1,0:T(8,128)S(1)}) custom-call(f32[8,8,128]{2,1,0:T(8,128)S(1)} %all-to-all-done.sums, f32[10,400,384]{2,1,0:T(8,128)S(1)} %copy-done.1, f32[8,400,384]{2,1,0:T(8,128)S(1)} %copy-done.6, f32[6,400,384]{2,1,0:T(8,128)S(1)} %copy-done.8, ...), custom_call_target="tpu_custom_call" | custom-call | tf_op jit(solution)/shard_map/terms/pallas_call | solution.py:455
  126.0 1.8 %collective-permute-start.4 = (f32[16,48,384]{2,1,0:T(8,128)S(1)}, f32[16,48,384]{2,1,0:T(8,128)S(1)}, u32[]{:S(2)}, u32[]{:S(2)}) collective-permute-start(f32[16,48,384]{2,1,0:T(8,128)S(1)} %get-tuple-element.27), channel_id=1, source_target_pairs={{0,8},{8,0},{16,24},{24,16},{32,40},{40,32},{48,56},{56,48},{64,72... | collective-permute-start | bytes 3538952 | tf_op jit(solution)/shard_map/ppermute | solution.py:469
  127.7 2.5 %collective-permute-done.4 = f32[16,48,384]{2,1,0:T(8,128)S(1)} collective-permute-done((f32[16,48,384]{2,1,0:T(8,128)S(1)}, f32[16,48,384]{2,1,0:T(8,128)S(1)}, u32[]{:S(2)}, u32[]{:S(2)}) %collective-permute-start.4) | collective-permute-done | bytes 1179680 | tf_op jit(solution)/shard_map/ppermute | solution.py:469
  130.2 0.2 add.17
  130.4 35.0 %all_to_all.10 = f32[16,48,384]{2,1,0:T(8,128)S(1)} all-to-all(f32[16,48,384]{2,1,0:T(8,128)S(1)} %add.17), channel_id=1, replica_groups={{0,16,32,48,64,80,96,112,128,144,160,176,192,208,224,240},{8,24,40,56,7..., dimensions={0} | all-to-all | bytes 2359296 | tf_op jit(solution)/shard_map/all_to_all | solution.py:473
  165.3 0.1 reduce_sum.19
  165.4 0.7 copy.9
  (5 shorter events, 0.1 us)
Async XLA Ops:
  7.2 18.9 %copy-start.4 = (f32[1,4,384,384]{3,2,1,0:T(8,128)S(1)}, f32[1,4,384,384]{3,2,1,0:T(8,128)}, u32[]{:S(2)}) copy-start(f32[1,4,384,384]{3,2,1,0:T(8,128)} %param.5) | copy-start | bytes 7077892
  7.2 63.6 %all-gather.2.cloned.1.call-start = ((), (), s32[]{:S(2)}) async-start(), calls=%async_computation.2 | async-start | bytes 5013504 | tf_op jit(solution)/shard_map/all_gather | solution.py:409
  8.8 23.5 %copy-start.12 = (f32[16]{0:T(128)S(1)}, f32[16]{0:T(128)}, u32[]{:S(2)}) copy-start(f32[16]{0:T(128)} %table.1) | copy-start | bytes 196
  10.8 9.1 %collective-permute-start.1 = (f32[105,384]{1,0:T(8,128)S(1)}, f32[105,384]{1,0:T(8,128)S(1)}, u32[]{:S(2)}, u32[]{:S(2)}) collective-permute-start(f32[105,384]{1,0:T(8,128)S(1)} %pad_maximum_fusion.1.own), channel_id=1, source_target_pairs={{0,7},{1,0},{2,1},{3,2},{4,3},{5,4},{6,5},{7,6},{8,15},{9,8},{10,9... | collective-permute-start | bytes 483848 | tf_op jit(solution)/shard_map/ppermute | solution.py:27
  16.8 8.5 %collective-permute-start = (f32[105,384]{1,0:T(8,128)S(1)}, f32[105,384]{1,0:T(8,128)S(1)}, u32[]{:S(2)}, u32[]{:S(2)}) collective-permute-start(f32[105,384]{1,0:T(8,128)S(1)} %pad_maximum_fusion.1.own), channel_id=1, source_target_pairs={{0,1},{1,2},{2,3},{3,4},{4,5},{5,6},{6,7},{7,0},{8,9},{9,10},{10,1... | collective-permute-start | bytes 483848 | tf_op jit(solution)/shard_map/ppermute | solution.py:27
  26.1 6.2 %copy-start.9 = (s32[4,384,384]{2,1,0:T(8,128)S(1)}, s32[4,384,384]{2,1,0:T(8,128)}, u32[]{:S(2)}) copy-start(s32[4,384,384]{2,1,0:T(8,128)} %classes.1) | copy-start | bytes 7077892
  27.2 79.3 %collective-permute-start.2 = (f32[1,384,384]{2,1,0:T(8,128)}, f32[1,384,384]{2,1,0:T(8,128)S(1)}, u32[]{:S(2)}, u32[]{:S(2)}) collective-permute-start(f32[1,384,384]{2,1,0:T(8,128)} %get-tuple-element.23), channel_id=1, source_target_pairs={{0,1},{1,2},{2,3},{3,4},{4,5},{5,6},{6,7},{7,0},{8,9},{9,10},{10,1... | collective-permute-start | bytes 1769480 | tf_op jit(solution)/shard_map/ppermute | solution.py:27
  28.9 77.6 %collective-permute-start.3 = (f32[1,384,384]{2,1,0:T(8,128)}, f32[1,384,384]{2,1,0:T(8,128)}, u32[]{:S(2)}, u32[]{:S(2)}) collective-permute-start(f32[1,384,384]{2,1,0:T(8,128)} %get-tuple-element.24), channel_id=1, source_target_pairs={{0,7},{1,0},{2,1},{3,2},{4,3},{5,4},{6,5},{7,6},{8,15},{9,8},{10,9... | collective-permute-start | bytes 1769480 | tf_op jit(solution)/shard_map/ppermute | solution.py:27
  48.8 2.5 %copy-start.2 = (f32[10,384,384]{2,1,0:T(8,128)}, f32[10,384,384]{2,1,0:T(8,128)S(1)}, u32[]{:S(2)}) copy-start(f32[10,384,384]{2,1,0:T(8,128)S(1)} %get-tuple-element.18.side) | copy-start | bytes 17694724
  51.3 1.4 copy-start.10
  70.8 2.7 %copy-start.3 = (f32[10,384,384]{2,1,0:T(8,128)S(1)}, f32[10,384,384]{2,1,0:T(8,128)}, u32[]{:S(2)}) copy-start(f32[10,384,384]{2,1,0:T(8,128)} %copy-done.2) | copy-start | bytes 17694724
  73.4 1.7 copy-start.11
  93.3 2.6 %copy-start = (f32[10,400,384]{2,1,0:T(8,128)}, f32[10,400,384]{2,1,0:T(8,128)S(1)}, u32[]{:S(2)}) copy-start(f32[10,400,384]{2,1,0:T(8,128)S(1)} %get-tuple-element.20.w0) | copy-start | bytes 18432004
  95.9 2.3 %copy-start.5 = (f32[8,400,384]{2,1,0:T(8,128)}, f32[8,400,384]{2,1,0:T(8,128)S(1)}, u32[]{:S(2)}) copy-start(f32[8,400,384]{2,1,0:T(8,128)S(1)} %get-tuple-element.21.w1) | copy-start | bytes 14745604
  98.2 1.9 %copy-start.7 = (f32[6,400,384]{2,1,0:T(8,128)}, f32[6,400,384]{2,1,0:T(8,128)S(1)}, u32[]{:S(2)}) copy-start(f32[6,400,384]{2,1,0:T(8,128)S(1)} %get-tuple-element.22.w2) | copy-start | bytes 11059204
  100.1 13.0 %all-to-all-start = ((f32[8,8,128]{2,1,0:T(8,128)}), f32[8,8,128]{2,1,0:T(8,128)S(1)}, u32[]{:S(2)}, u32[]{:S(2)}) async-start(f32[8,8,128]{2,1,0:T(8,128)} %get-tuple-element.19), calls=%async_computation | async-start | bytes 65536 | tf_op jit(solution)/shard_map/all_to_all | solution.py:453
  113.1 2.7 %copy-start.1 = (f32[10,400,384]{2,1,0:T(8,128)S(1)}, f32[10,400,384]{2,1,0:T(8,128)}, u32[]{:S(2)}) copy-start(f32[10,400,384]{2,1,0:T(8,128)} %copy-done) | copy-start | bytes 18432004
  115.8 2.4 %copy-start.6 = (f32[8,400,384]{2,1,0:T(8,128)S(1)}, f32[8,400,384]{2,1,0:T(8,128)}, u32[]{:S(2)}) copy-start(f32[8,400,384]{2,1,0:T(8,128)} %copy-done.5) | copy-start | bytes 14745604
  118.2 2.0 %copy-start.8 = (f32[6,400,384]{2,1,0:T(8,128)S(1)}, f32[6,400,384]{2,1,0:T(8,128)}, u32[]{:S(2)}) copy-start(f32[6,400,384]{2,1,0:T(8,128)} %copy-done.7) | copy-start | bytes 11059204
  126.0 4.2 %collective-permute-start.4 = (f32[16,48,384]{2,1,0:T(8,128)S(1)}, f32[16,48,384]{2,1,0:T(8,128)S(1)}, u32[]{:S(2)}, u32[]{:S(2)}) collective-permute-start(f32[16,48,384]{2,1,0:T(8,128)S(1)} %get-tuple-element.27), channel_id=1, source_target_pairs={{0,8},{8,0},{16,24},{24,16},{32,40},{40,32},{48,56},{56,48},{64,72... | collective-permute-start | bytes 3538952 | tf_op jit(solution)/shard_map/ppermute | solution.py:469
Sparse Core Ops, SparseCore 0:
  26.2 44.4 all-gather.1

commit v4 on v3

--- a/solution.py
+++ b/solution.py
@@ -104,7 +104,7 @@
 
 
 def vectors_kernel(
-    own, halo, side, f0, f1, f2, sums, cond, near_x, near_y, near_z, inverse, marks
+    own, halo, right, f0, f1, f2, sums, cond, side, near_x, near_y, near_z, inverse, marks
 ):
     layers, rows, columns = own.shape
     blocks, _, _, strip, _ = halo.shape
@@ -118,10 +118,14 @@
         group.append(copy)
 
     fetch(own, cond.at[pl.ds(layers, layers), filled], first_copies)
+    inner = pl.ds(REACH, layers)
+    fetch(right.at[inner], side.at[inner], first_copies)
     for block in range(blocks):
         for step in range(2):
             target = cond.at[pl.ds(2 * step * layers, layers), pl.ds(PAD + block * strip, strip)]
             fetch(halo.at[block, step], target, copies)
+    for ends in (pl.ds(0, REACH), pl.ds(REACH + layers, REACH)):
+        fetch(right.at[ends], side.at[ends], copies)
     slab = lax.axis_index("slab")
     slabs = lax.axis_size("slab")
     deep = layers + 2 * REACH
@@ -420,12 +424,13 @@
     deep = layers + 2 * REACH
     side, own = pl.pallas_call(
         scatter_kernel,
-        out_shape=(kept(deep, rows, columns), kept(layers, rows, columns)),
+        out_shape=(struct(deep, rows, columns), struct(layers, rows, columns)),
         in_specs=[vmem, vmem, vmem, vmem, smem],
         compiler_params=limit(24),
         name="scatter",
     )(below, packed, above, classes, table)
 
+    halo, lower, upper = lax.optimization_barrier((halo, lower, upper))
     tall = rows + 2 * PAD
     thick = layers + 2
     w0, w1, w2, sums = pl.pallas_call(
@@ -436,19 +441,20 @@
             kept(deep - 4, tall, columns),
             struct(count, 8, 128),
         ),
-        in_specs=[vmem, anywhere, vmem],
+        in_specs=[anywhere] * 3,
         out_specs=(vmem, vmem, vmem, vmem),
         scratch_shapes=[
             pltpu.VMEM((deep + 2, tall, columns), jnp.float32),
             pltpu.VMEM((deep, rows, columns), jnp.float32),
+            pltpu.VMEM((deep, rows, columns), jnp.float32),
             pltpu.VMEM((deep, tall, columns), jnp.float32),
             pltpu.VMEM((deep, rows, columns), jnp.float32),
             pltpu.VMEM((deep, rows, columns), jnp.float32),
-            pltpu.SemaphoreType.DMA((2 * blocks + 1,)),
+            pltpu.SemaphoreType.DMA((2 * blocks + 4,)),
         ],
-        compiler_params=limit(34),
+        compiler_params=limit(40),
         name="vectors",
-    )(stay(own), halo, stay(side))
+    )(own, halo, side)
 
     sums = lax.all_to_all(sums, "slab", 0, 0)
     half = rows // sources
@@ -467,10 +473,27 @@
     )(sums, stay(w0), stay(w1), stay(w2), forward, lower, upper)
 
     got = lax.ppermute(give, "src", [(i, i ^ 1) for i in range(sources)])
+    both = (keep + got).reshape(depth // 2, 2, Y_LO, layers * half, columns)
+    parity = (place // per_z) % 2
+    held = lax.dynamic_index_in_dim(both, parity, 1, keepdims=False)
+    sent = lax.dynamic_index_in_dim(both, 1 - parity, 1, keepdims=False)
+
+    def beside(value, way):
+        pairs = []
+        for i in range(sources):
+            step = way if (i // per_z) % 2 == 0 else -way
+            pairs.append((i, (i + step * per_z) % sources))
+        return lax.ppermute(value, "src", pairs)
+
+    middle = layers * half // 2
+    came = [beside(sent[:, :, :middle], 1), beside(sent[:, :, middle:], -1)]
+    part = (held + jnp.concatenate(came, axis=2)).reshape(blocks // 2, layers * half, columns)
     groups = [
-        [z * per_z + y * CORES + c for z in range(depth) for y in range(Y_LO)] for c in range(CORES)
+        [z * per_z + y * CORES + c for z in range(first, depth, 2) for y in range(Y_LO)]
+        for first in range(2)
+        for c in range(CORES)
     ]
-    shares = lax.all_to_all(keep + got, "src", 0, 0, axis_index_groups=groups)
+    shares = lax.all_to_all(part, "src", 0, 0, axis_index_groups=groups)
     gradient = jnp.sum(shares, axis=0).reshape(layers, half, columns)
     return (adjoint[None], gradient)
 

time: 173 us -> 154 us (0.89)
  local copies, waits for them, and re-layouts: 25 us -> 7.4 us
  starting transfers between devices: 19.3 us -> 15.5 us
  Pallas kernels: 40.3 us -> 43.4 us
    unnamed x27 -> x19, local copies, waits for them, and re-layouts: 22.9 us -> 6.25 us
    ppermute x0 -> x2, waiting for transfers between devices: none -> 7.57 us  [beside(): return lax.ppermute(value, 'src', pairs)]
    all_to_all x1 -> x0, waiting for transfers between devices: 6.55 us -> none  [body(): sums = lax.all_to_all(sums, 'slab', 0, 0)]
    all_to_all x1 -> x0, starting transfers between devices: 6.43 us -> none  [body(): sums = lax.all_to_all(sums, 'slab', 0, 0)]
    ppermute x0 -> x2, starting transfers between devices: none -> 2.47 us  [beside(): return lax.ppermute(value, 'src', pairs)]
    all_gather x1, waiting for transfers between devices: 18 us -> 15.6 us  [body(): halo = lax.all_gather(shares, 'src', axis_index_groups=groups)]
    pallas_call x1, Pallas kernels: 18.1 us -> 20.5 us  [body(): pl.pallas_call(vectors_kernel, out_shape=(kept(deep, tall, columns), kept...]
    all_to_all x1 -> x2, blocking collectives: 35 us -> 33.7 us  [the longest x1 20.9 us: body(): shares = lax.all_to_all(part, 'src', 0, 0, axis_index_groups=groups)]
  transfers between devices with their start and end apart: 7 -> 8, of which waited for: 5 -> 7; matrix products, arithmetic and copies ran while one was open for 1% -> 0% of each run, Pallas kernels for 20% -> 11%
where the time goes in v4:
time: 154 us; the launch traced here: 153 us
  Pallas kernels  43.4 us (28%)
  waiting for transfers between devices  35.4 us (23%)
  blocking collectives  33.7 us (22%)
  starting transfers between devices  15.5 us (10%)
  between operations  14.2 us (9%)
  local copies, waits for them, and re-layouts  7.4 us (5%)
  other arithmetic  3.5 us (2%)
    all_to_all x1, blocking collectives, body(): shares = lax.all_to_all(part, 'src', 0, 0, axis_index_groups=groups)  20.9 us
    pallas_call x1, Pallas kernels, body(): pl.pallas_call(vectors_kernel, out_shape=(kept(deep, tall, columns), kept...  20.5 us
    pallas_call x1, Pallas kernels, body(): pl.pallas_call(scatter_kernel, out_shape=(struct(deep, rows, columns), st...  16.5 us
    all_gather x1, waiting for transfers between devices, body(): halo = lax.all_gather(shares, 'src', axis_index_groups=groups)  15.6 us
    all_to_all x1, blocking collectives, body(): sums = lax.all_to_all(sums, 'slab', 0, 0)  12.8 us
    ppermute x4, starting transfers between devices, slab_ring(): lax.ppermute(value, 'slab', [(i, (i + step) % count) for i in range(count)])  11.3 us
    ppermute x4, waiting for transfers between devices, slab_ring(): lax.ppermute(value, 'slab', [(i, (i + step) % count) for i in range(count)])  9.58 us
    ppermute x2, waiting for transfers between devices, beside(): return lax.ppermute(value, 'src', pairs)  7.57 us
  transfers between devices with their start and end apart: 8, of which 7 were waited for; matrix products, arithmetic and copies ran while one was open for 0% of the time, Pallas kernels for 11%

profile of v4, /device:TPU:1, one launch (start us, length us, event | category | flops | bytes accessed | tf_op | source)
XLA Modules:
  0.0 153.2 jit_solution(18435969211924484992)
XLA Ops:
  7.2 0.0 copy-start.1
  7.2 0.0 all-gather.2.cloned.1.call-start
  7.2 0.9 convert_bitcast_fusion
  8.1 0.7 pad_maximum_fusion.2
  8.8 0.0 copy-start.8
  8.8 0.9 constant_dynamic-slice_fusion.1
  9.8 1.0 select_reduce_fusion
  10.8 3.8 %collective-permute-start = (f32[105,384]{1,0:T(8,128)S(1)}, f32[105,384]{1,0:T(8,128)S(1)}, u32[]{:S(2)}, u32[]{:S(2)}) collective-permute-start(f32[105,384]{1,0:T(8,128)S(1)} %pad_maximum_fusion.1.own), channel_id=1, source_target_pairs={{0,1},{1,2},{2,3},{3,4},{4,5},{5,6},{6,7},{7,0},{8,9},{9,10},{10,1... | collective-permute-start | bytes 483848 | tf_op jit(solution)/shard_map/ppermute | solution.py:27
  14.6 2.3 %collective-permute-start.1 = (f32[105,384]{1,0:T(8,128)S(1)}, f32[105,384]{1,0:T(8,128)S(1)}, u32[]{:S(2)}, u32[]{:S(2)}) collective-permute-start(f32[105,384]{1,0:T(8,128)S(1)} %pad_maximum_fusion.1.own), channel_id=1, source_target_pairs={{0,7},{1,0},{2,1},{3,2},{4,3},{5,4},{6,5},{7,6},{8,15},{9,8},{10,9... | collective-permute-start | bytes 483848 | tf_op jit(solution)/shard_map/ppermute | solution.py:27
  16.9 4.3 %collective-permute-done.below = f32[105,384]{1,0:T(8,128)S(1)} collective-permute-done((f32[105,384]{1,0:T(8,128)S(1)}, f32[105,384]{1,0:T(8,128)S(1)}, u32[]{:S(2)}, u32[]{:S(2)}) %collective-permute-start) | collective-permute-done | bytes 161312 | tf_op jit(solution)/shard_map/ppermute | solution.py:27
  21.2 3.9 %collective-permute-done.1.above = f32[105,384]{1,0:T(8,128)S(1)} collective-permute-done((f32[105,384]{1,0:T(8,128)S(1)}, f32[105,384]{1,0:T(8,128)S(1)}, u32[]{:S(2)}, u32[]{:S(2)}) %collective-permute-start.1) | collective-permute-done | bytes 161312 | tf_op jit(solution)/shard_map/ppermute | solution.py:27
  25.1 0.7 pad_maximum_fusion
  25.8 0.0 all-gather.2.cloned.1.call-update
  25.8 0.0 copy-done.1
  25.8 0.0 copy-start.2
  25.8 0.1 slice_bitcast_fusion
  25.9 0.1 collective-permute-start.2
  26.0 5.1 %collective-permute-start.3 = (f32[1,384,384]{2,1,0:T(8,128)S(1)}, f32[1,384,384]{2,1,0:T(8,128)S(1)}, u32[]{:S(2)}, u32[]{:S(2)}) collective-permute-start(f32[1,384,384]{2,1,0:T(8,128)S(1)} %get-tuple-element.22), channel_id=1, source_target_pairs={{0,7},{1,0},{2,1},{3,2},{4,3},{5,4},{6,5},{7,6},{8,15},{9,8},{10,9... | collective-permute-start | bytes 1769480 | tf_op jit(solution)/shard_map/ppermute | solution.py:27
  31.1 0.0 copy-done.8
  31.1 0.0 copy-done.2
  31.1 16.5 %scatter.1 = (f32[10,384,384]{2,1,0:T(8,128)S(1)}, f32[4,384,384]{2,1,0:T(8,128)S(1)}) custom-call(f32[105,384]{1,0:T(8,128)S(1)} %collective-permute-done.below, f32[105,384]{1,0:T(8,128)S(1)} %pad_maximum_fusion.1.own, f32[105,384]{1,0:T(8,128)S(1)} %collective-permute-done.1.above, s32[4,384,384]{2,1,0:T(8,128)S(1)} %copy-done.2, f32[16]{0:T(128)S(1)} %copy-done.8), custom_call_target="tpu_custom_call" | custom-call | tf_op jit(solution)/shard_map/scatter/pallas_call | solution.py:425
  47.6 0.0 copy-start
  47.6 2.5 %copy-done = f32[10,384,384]{2,1,0:T(8,128)} copy-done((f32[10,384,384]{2,1,0:T(8,128)}, f32[10,384,384]{2,1,0:T(8,128)S(1)}, u32[]{:S(2)}) %copy-start) | copy-done | bytes 5898264
  50.1 0.0 copy-start.3
  50.1 1.4 copy-done.3
  51.5 0.0 collective-permute-done.2.lower
  51.5 0.0 copy-start.4
  51.5 0.8 copy-done.4
  52.4 1.4 collective-permute-done.3.upper
  53.8 0.0 copy-start.6
  53.8 0.8 copy-done.6
  54.6 15.6 %all-gather.2.cloned.1.call-done.halo = f32[16,2,4,24,384]{4,3,2,1,0:T(8,128)} async-done(((f32[1,2,4,24,384]{4,3,2,1,0:T(8,128)}), f32[16,2,4,24,384]{4,3,2,1,0:T(8,128)}) %all-gather.2.cloned.1.call-update) | async-done | bytes 4718608 | tf_op jit(solution)/shard_map/all_gather | solution.py:413
  70.1 0.0 copy-start.5
  70.1 0.0 copy-start.7
  70.1 20.5 %vectors.1 = (f32[10,400,384]{2,1,0:T(8,128)S(1)}, f32[8,400,384]{2,1,0:T(8,128)S(1)}, f32[6,400,384]{2,1,0:T(8,128)S(1)}, f32[8,8,128]{2,1,0:T(8,128)}) custom-call(f32[4,384,384]{2,1,0:T(8,128)} %copy-done.3, f32[16,2,4,24,384]{4,3,2,1,0:T(8,128)} %all-gather.2.cloned.1.call-done.halo, f32[10,384,384]{2,1,0:T(8,128)} %copy-done), custom_call_target="tpu_custom_call" | custom-call | tf_op jit(solution)/shard_map/vectors/pallas_call | solution.py:436
  90.6 12.8 %all_to_all.10.sums = f32[8,8,128]{2,1,0:T(8,128)S(1)} all-to-all(f32[8,8,128]{2,1,0:T(8,128)} %get-tuple-element.25), channel_id=1, replica_groups=mesh['src'=32,'slab'=8] {'slab'}, dimensions={0} | all-to-all | bytes 65536 | tf_op jit(solution)/shard_map/all_to_all | solution.py:459
  103.4 0.0 copy-done.5
  103.4 0.0 copy-done.7
  103.4 6.5 %terms.1 = (f32[4,384,384]{2,1,0:T(8,128)}, f32[16,48,384]{2,1,0:T(8,128)S(1)}, f32[16,48,384]{2,1,0:T(8,128)}) custom-call(f32[8,8,128]{2,1,0:T(8,128)S(1)} %all_to_all.10.sums, f32[10,400,384]{2,1,0:T(8,128)S(1)} %get-tuple-element.26.w0, f32[8,400,384]{2,1,0:T(8,128)S(1)} %get-tuple-element.27.w1, f32[6,400,384]{2,1,0:T(8,128)S(1)} %get-tuple-element.28.w2, ...), custom_call_target="tpu_custom_call" | custom-call | tf_op jit(solution)/shard_map/terms/pallas_call | solution.py:461
  109.9 1.8 %collective-permute-start.4 = (f32[16,48,384]{2,1,0:T(8,128)}, f32[16,48,384]{2,1,0:T(8,128)S(1)}, u32[]{:S(2)}, u32[]{:S(2)}) collective-permute-start(f32[16,48,384]{2,1,0:T(8,128)} %get-tuple-element.33), channel_id=1, source_target_pairs={{0,8},{8,0},{16,24},{24,16},{32,40},{40,32},{48,56},{56,48},{64,72... | collective-permute-start | bytes 3538952 | tf_op jit(solution)/shard_map/ppermute | solution.py:475
  111.7 2.7 %collective-permute-done.4 = f32[16,48,384]{2,1,0:T(8,128)S(1)} collective-permute-done((f32[16,48,384]{2,1,0:T(8,128)}, f32[16,48,384]{2,1,0:T(8,128)S(1)}, u32[]{:S(2)}, u32[]{:S(2)}) %collective-permute-start.4) | collective-permute-done | bytes 1179680 | tf_op jit(solution)/shard_map/ppermute | solution.py:475
  114.3 0.1 add.32
  114.5 0.1 constant_dynamic-slice_fusion
  114.6 0.9 collective-permute-start.5
  115.5 1.5 %collective-permute-start.6 = (f32[4,2,24,384]{3,2,1,0:T(8,128)S(1)}, f32[4,2,24,384]{3,2,1,0:T(8,128)S(1)}, u32[]{:S(2)}, u32[]{:S(2)}) collective-permute-start(f32[4,2,24,384]{3,2,1,0:T(8,128)S(1)} %get-tuple-element.45), channel_id=1, source_target_pairs={{0,224},{8,232},{16,240},{24,248},{32,64},{40,72},{48,80},{56,88},... | collective-permute-start | bytes 884744 | tf_op jit(solution)/shard_map/ppermute | solution.py:486
  117.1 5.8 %collective-permute-done.5 = f32[4,2,24,384]{3,2,1,0:T(8,128)S(1)} collective-permute-done((f32[4,2,24,384]{3,2,1,0:T(8,128)S(1)}, f32[4,2,24,384]{3,2,1,0:T(8,128)S(1)}, u32[]{:S(2)}, u32[]{:S(2)}) %collective-permute-start.5) | collective-permute-done | bytes 294944 | tf_op jit(solution)/shard_map/ppermute | solution.py:486
  122.9 1.7 %collective-permute-done.6 = f32[4,2,24,384]{3,2,1,0:T(8,128)S(1)} collective-permute-done((f32[4,2,24,384]{3,2,1,0:T(8,128)S(1)}, f32[4,2,24,384]{3,2,1,0:T(8,128)S(1)}, u32[]{:S(2)}, u32[]{:S(2)}) %collective-permute-start.6) | collective-permute-done | bytes 294944 | tf_op jit(solution)/shard_map/ppermute | solution.py:486
  124.7 0.1 maximum_add_fusion
  124.7 20.9 %all_to_all.11 = f32[8,48,384]{2,1,0:T(8,128)S(1)} all-to-all(f32[8,48,384]{2,1,0:T(8,128)S(1)} %maximum_add_fusion), channel_id=1, replica_groups={{0,16,64,80,128,144,192,208},{8,24,72,88,136,152,200,216},{32,48,96,112..., dimensions={0} | all-to-all | bytes 1179648 | tf_op jit(solution)/shard_map/all_to_all | solution.py:496
  145.7 0.7 copy.9
  (7 shorter events, 0.1 us)
Async XLA Ops:
  7.2 18.7 %copy-start.1 = (f32[1,4,384,384]{3,2,1,0:T(8,128)S(1)}, f32[1,4,384,384]{3,2,1,0:T(8,128)}, u32[]{:S(2)}) copy-start(f32[1,4,384,384]{3,2,1,0:T(8,128)} %param.5) | copy-start | bytes 7077892
  7.2 63.0 %all-gather.2.cloned.1.call-start = ((), (), s32[]{:S(2)}) async-start(), calls=%async_computation.2 | async-start | bytes 5013504 | tf_op jit(solution)/shard_map/all_gather | solution.py:413
  8.8 22.3 %copy-start.8 = (f32[16]{0:T(128)S(1)}, f32[16]{0:T(128)}, u32[]{:S(2)}) copy-start(f32[16]{0:T(128)} %table.1) | copy-start | bytes 196
  10.8 10.4 %collective-permute-start = (f32[105,384]{1,0:T(8,128)S(1)}, f32[105,384]{1,0:T(8,128)S(1)}, u32[]{:S(2)}, u32[]{:S(2)}) collective-permute-start(f32[105,384]{1,0:T(8,128)S(1)} %pad_maximum_fusion.1.own), channel_id=1, source_target_pairs={{0,1},{1,2},{2,3},{3,4},{4,5},{5,6},{6,7},{7,0},{8,9},{9,10},{10,1... | collective-permute-start | bytes 483848 | tf_op jit(solution)/shard_map/ppermute | solution.py:27
  14.6 10.5 %collective-permute-start.1 = (f32[105,384]{1,0:T(8,128)S(1)}, f32[105,384]{1,0:T(8,128)S(1)}, u32[]{:S(2)}, u32[]{:S(2)}) collective-permute-start(f32[105,384]{1,0:T(8,128)S(1)} %pad_maximum_fusion.1.own), channel_id=1, source_target_pairs={{0,7},{1,0},{2,1},{3,2},{4,3},{5,4},{6,5},{7,6},{8,15},{9,8},{10,9... | collective-permute-start | bytes 483848 | tf_op jit(solution)/shard_map/ppermute | solution.py:27
  25.8 5.3 %copy-start.2 = (s32[4,384,384]{2,1,0:T(8,128)S(1)}, s32[4,384,384]{2,1,0:T(8,128)}, u32[]{:S(2)}) copy-start(s32[4,384,384]{2,1,0:T(8,128)} %classes.1) | copy-start | bytes 7077892
  25.9 25.6 %collective-permute-start.2 = (f32[1,384,384]{2,1,0:T(8,128)S(1)}, f32[1,384,384]{2,1,0:T(8,128)S(1)}, u32[]{:S(2)}, u32[]{:S(2)}) collective-permute-start(f32[1,384,384]{2,1,0:T(8,128)S(1)} %get-tuple-element.21), channel_id=1, source_target_pairs={{0,1},{1,2},{2,3},{3,4},{4,5},{5,6},{6,7},{7,0},{8,9},{9,10},{10,1... | collective-permute-start | bytes 1769480 | tf_op jit(solution)/shard_map/ppermute | solution.py:27
  26.0 27.7 %collective-permute-start.3 = (f32[1,384,384]{2,1,0:T(8,128)S(1)}, f32[1,384,384]{2,1,0:T(8,128)S(1)}, u32[]{:S(2)}, u32[]{:S(2)}) collective-permute-start(f32[1,384,384]{2,1,0:T(8,128)S(1)} %get-tuple-element.22), channel_id=1, source_target_pairs={{0,7},{1,0},{2,1},{3,2},{4,3},{5,4},{6,5},{7,6},{8,15},{9,8},{10,9... | collective-permute-start | bytes 1769480 | tf_op jit(solution)/shard_map/ppermute | solution.py:27
  47.6 2.5 %copy-start = (f32[10,384,384]{2,1,0:T(8,128)}, f32[10,384,384]{2,1,0:T(8,128)S(1)}, u32[]{:S(2)}) copy-start(f32[10,384,384]{2,1,0:T(8,128)S(1)} %get-tuple-element.24.right) | copy-start | bytes 17694724
  50.1 1.4 copy-start.3
  51.5 0.8 copy-start.4
  53.8 0.8 copy-start.6
  70.1 33.2 %copy-start.5 = (f32[1,384,384]{2,1,0:T(8,128)S(1)}, f32[1,384,384]{2,1,0:T(8,128)}, u32[]{:S(2)}) copy-start(f32[1,384,384]{2,1,0:T(8,128)} %copy-done.4) | copy-start | bytes 1769476
  70.1 33.2 %copy-start.7 = (f32[1,384,384]{2,1,0:T(8,128)S(1)}, f32[1,384,384]{2,1,0:T(8,128)}, u32[]{:S(2)}) copy-start(f32[1,384,384]{2,1,0:T(8,128)} %copy-done.6) | copy-start | bytes 1769476
  109.9 4.5 %collective-permute-start.4 = (f32[16,48,384]{2,1,0:T(8,128)}, f32[16,48,384]{2,1,0:T(8,128)S(1)}, u32[]{:S(2)}, u32[]{:S(2)}) collective-permute-start(f32[16,48,384]{2,1,0:T(8,128)} %get-tuple-element.33), channel_id=1, source_target_pairs={{0,8},{8,0},{16,24},{24,16},{32,40},{40,32},{48,56},{56,48},{64,72... | collective-permute-start | bytes 3538952 | tf_op jit(solution)/shard_map/ppermute | solution.py:475
  114.6 8.3 %collective-permute-start.5 = (f32[4,2,24,384]{3,2,1,0:T(8,128)S(1)}, f32[4,2,24,384]{3,2,1,0:T(8,128)S(1)}, u32[]{:S(2)}, u32[]{:S(2)}) collective-permute-start(f32[4,2,24,384]{3,2,1,0:T(8,128)S(1)} %get-tuple-element.44), channel_id=1, source_target_pairs={{0,32},{8,40},{16,48},{24,56},{32,0},{40,8},{48,16},{56,24},{64,96... | collective-permute-start | bytes 884744 | tf_op jit(solution)/shard_map/ppermute | solution.py:486
  115.5 9.1 %collective-permute-start.6 = (f32[4,2,24,384]{3,2,1,0:T(8,128)S(1)}, f32[4,2,24,384]{3,2,1,0:T(8,128)S(1)}, u32[]{:S(2)}, u32[]{:S(2)}) collective-permute-start(f32[4,2,24,384]{3,2,1,0:T(8,128)S(1)} %get-tuple-element.45), channel_id=1, source_target_pairs={{0,224},{8,232},{16,240},{24,248},{32,64},{40,72},{48,80},{56,88},... | collective-permute-start | bytes 884744 | tf_op jit(solution)/shard_map/ppermute | solution.py:486
Sparse Core Ops, SparseCore 0:
  25.9 44.1 all-gather.1

commit v5 on v4

--- a/solution.py
+++ b/solution.py
@@ -395,12 +395,9 @@
 
     mine = (place // per_z) * CORES + core
     part = lookup(lax.dynamic_slice_in_dim(classes, mine * strip, strip, axis=1), table)
-    lists = jnp.concatenate([receivers[0].T.astype(jnp.float32), misfit], axis=0)
-    packed = jnp.concatenate(
-        [part.reshape(layers * strip, columns), lists.reshape(3 * PIECES, columns)], axis=0
-    )
-    below = slab_ring(packed, 1)
-    above = slab_ring(packed, -1)
+    part = part.reshape(layers * strip, columns)
+    below = slab_ring(part, 1)
+    above = slab_ring(part, -1)
     shares = jnp.stack(
         [
             jnp.where(slab > 0, below[: layers * strip], 0.0),
@@ -411,6 +408,12 @@
         [z * per_z + y * CORES + c for z in range(depth) for c in range(CORES)] for y in range(Y_LO)
     ]
     halo = lax.all_gather(shares, "src", axis_index_groups=groups)
+
+    entries, weight, below, above = lax.optimization_barrier((receivers, misfit, below, above))
+    lists = jnp.concatenate([entries[0].T.astype(jnp.float32), weight], axis=0)
+    packed = lists.reshape(3 * PIECES, columns)
+    below = slab_ring(packed, 1)
+    above = slab_ring(packed, -1)
 
     bottom, top, below, above = lax.optimization_barrier(
         (forward[:1], forward[-1:], below, above)

time: 154 us -> 151 us (0.981)
  waiting for transfers between devices: 35.4 us -> 27.2 us
  starting transfers between devices: 15.5 us -> 20.5 us
    all_gather x1, waiting for transfers between devices: 15.6 us -> 6.19 us  [body(): halo = lax.all_gather(shares, 'src', axis_index_groups=groups)]
    ppermute x4 -> x6, starting transfers between devices: 11.3 us -> 16.4 us  [slab_ring(): lax.ppermute(value, 'slab', [(i, (i + step) % count) for i in range(count)])]
    ppermute x4 -> x6, waiting for transfers between devices: 9.58 us -> 11 us  [slab_ring(): lax.ppermute(value, 'slab', [(i, (i + step) % count) for i in range(count)])]
    unnamed x19 -> x15, local copies, waits for them, and re-layouts: 6.25 us -> 5.34 us
  transfers between devices with their start and end apart: 8 -> 10, of which waited for: 7 -> 7; matrix products, arithmetic and copies ran while one was open for 0% -> 2% of each run, Pallas kernels for 11% -> 11%
where the time goes in v5:
time: 151 us
  Pallas kernels  43.5 us (29%)
  blocking collectives  34.4 us (23%)
  waiting for transfers between devices  27.2 us (18%)
  starting transfers between devices  20.5 us (14%)
  between operations  14.2 us (9%)
  local copies, waits for them, and re-layouts  7.89 us (5%)
  other arithmetic  3.34 us (2%)
    all_to_all x1, blocking collectives, body(): shares = lax.all_to_all(part, 'src', 0, 0, axis_index_groups=groups)  21.3 us
    pallas_call x1, Pallas kernels, body(): pl.pallas_call(vectors_kernel, out_shape=(kept(deep, tall, columns), kept...  20.5 us
    pallas_call x1, Pallas kernels, body(): pl.pallas_call(scatter_kernel, out_shape=(struct(deep, rows, columns), st...  16.5 us
    ppermute x6, starting transfers between devices, slab_ring(): lax.ppermute(value, 'slab', [(i, (i + step) % count) for i in range(count)])  16.4 us
    all_to_all x1, blocking collectives, body(): sums = lax.all_to_all(sums, 'slab', 0, 0)  13.1 us
    ppermute x6, waiting for transfers between devices, slab_ring(): lax.ppermute(value, 'slab', [(i, (i + step) % count) for i in range(count)])  11 us
    ppermute x2, waiting for transfers between devices, beside(): return lax.ppermute(value, 'src', pairs)  7.3 us
    pallas_call x1, Pallas kernels, body(): pl.pallas_call(terms_kernel, out_shape=(struct(layers, rows, columns),) +...  6.48 us
  transfers between devices with their start and end apart: 10, of which 7 were waited for; matrix products, arithmetic and copies ran while one was open for 2% of the time, Pallas kernels for 11%

profile of v5, /device:TPU:1, one launch (start us, length us, event | category | flops | bytes accessed | tf_op | source)
XLA Modules:
  0.0 151.0 jit_solution(18322229024859984690)
XLA Ops:
  7.2 0.0 copy-start.2
  7.2 0.0 copy-start.6
  7.2 0.0 all-gather.2.cloned.1.call-start
  7.3 1.1 constant_dynamic-slice_fusion.1
  8.3 1.0 select_reduce_fusion
  9.3 3.8 %collective-permute-start = (f32[96,384]{1,0:T(8,128)S(1)}, f32[96,384]{1,0:T(8,128)S(1)}, u32[]{:S(2)}, u32[]{:S(2)}) collective-permute-start(f32[96,384]{1,0:T(8,128)S(1)} %bitcast.26), channel_id=1, source_target_pairs={{0,1},{1,2},{2,3},{3,4},{4,5},{5,6},{6,7},{7,0},{8,9},{9,10},{10,1... | collective-permute-start | bytes 442376 | tf_op jit(solution)/shard_map/ppermute | solution.py:27
  13.1 2.3 %collective-permute-start.1 = (f32[96,384]{1,0:T(8,128)S(1)}, f32[96,384]{1,0:T(8,128)S(1)}, u32[]{:S(2)}, u32[]{:S(2)}) collective-permute-start(f32[96,384]{1,0:T(8,128)S(1)} %bitcast.27), channel_id=1, source_target_pairs={{0,7},{1,0},{2,1},{3,2},{4,3},{5,4},{6,5},{7,6},{8,15},{9,8},{10,9... | collective-permute-start | bytes 442376 | tf_op jit(solution)/shard_map/ppermute | solution.py:27
  15.4 2.5 %collective-permute-done = f32[96,384]{1,0:T(8,128)S(1)} collective-permute-done((f32[96,384]{1,0:T(8,128)S(1)}, f32[96,384]{1,0:T(8,128)S(1)}, u32[]{:S(2)}, u32[]{:S(2)}) %collective-permute-start) | collective-permute-done | bytes 147488 | tf_op jit(solution)/shard_map/ppermute | solution.py:27
  18.0 4.3 %collective-permute-done.1 = f32[96,384]{1,0:T(8,128)S(1)} collective-permute-done((f32[96,384]{1,0:T(8,128)S(1)}, f32[96,384]{1,0:T(8,128)S(1)}, u32[]{:S(2)}, u32[]{:S(2)}) %collective-permute-start.1) | collective-permute-done | bytes 147488 | tf_op jit(solution)/shard_map/ppermute | solution.py:27
  22.2 0.7 pad_maximum_fusion
  23.0 0.0 all-gather.2.cloned.1.call-update
  23.0 0.7 convert_bitcast_fusion
  23.7 0.7 pad_maximum_fusion.1
  24.4 0.0 copy-start.4
  24.4 0.4 collective-permute-start.2
  24.8 4.8 %collective-permute-start.3 = (f32[9,384]{1,0:T(8,128)S(1)}, f32[9,384]{1,0:T(8,128)S(1)}, u32[]{:S(2)}, u32[]{:S(2)}) collective-permute-start(f32[9,384]{1,0:T(8,128)S(1)} %reshape.30.own), channel_id=1, source_target_pairs={{0,7},{1,0},{2,1},{3,2},{4,3},{5,4},{6,5},{7,6},{8,15},{9,8},{10,9... | collective-permute-start | bytes 41480 | tf_op jit(solution)/shard_map/ppermute | solution.py:27
  29.6 1.3 slice_bitcast_fusion
  30.9 0.0 collective-permute-done.2.below
  30.9 0.0 collective-permute-done.3.above
  30.9 0.0 copy-done.4
  31.0 1.7 %collective-permute-start.4 = (f32[1,384,384]{2,1,0:T(8,128)S(1)}, f32[1,384,384]{2,1,0:T(8,128)S(1)}, u32[]{:S(2)}, u32[]{:S(2)}) collective-permute-start(f32[1,384,384]{2,1,0:T(8,128)S(1)} %get-tuple-element.25), channel_id=1, source_target_pairs={{0,1},{1,2},{2,3},{3,4},{4,5},{5,6},{6,7},{7,0},{8,9},{9,10},{10,1... | collective-permute-start | bytes 1769480 | tf_op jit(solution)/shard_map/ppermute | solution.py:27
  32.6 3.5 %collective-permute-start.5 = (f32[1,384,384]{2,1,0:T(8,128)S(1)}, f32[1,384,384]{2,1,0:T(8,128)S(1)}, u32[]{:S(2)}, u32[]{:S(2)}) collective-permute-start(f32[1,384,384]{2,1,0:T(8,128)S(1)} %get-tuple-element.26), channel_id=1, source_target_pairs={{0,7},{1,0},{2,1},{3,2},{4,3},{5,4},{6,5},{7,6},{8,15},{9,8},{10,9... | collective-permute-start | bytes 1769480 | tf_op jit(solution)/shard_map/ppermute | solution.py:27
  36.1 0.0 copy-done.2
  36.1 0.0 copy-done.6
  36.1 0.0 copy-start.5
  36.1 0.7 copy-done.5
  36.9 16.5 %scatter.1 = (f32[10,384,384]{2,1,0:T(8,128)S(1)}, f32[4,384,384]{2,1,0:T(8,128)S(1)}) custom-call(f32[9,384]{1,0:T(8,128)S(1)} %collective-permute-done.2.below, f32[9,384]{1,0:T(8,128)S(1)} %copy-done.5, f32[9,384]{1,0:T(8,128)S(1)} %collective-permute-done.3.above, s32[4,384,384]{2,1,0:T(8,128)S(1)} %copy-done.2, f32[16]{0:T(128)S(1)} %copy-done.6), custom_call_target="tpu_custom_call" | custom-call | tf_op jit(solution)/shard_map/scatter/pallas_call | solution.py:428
  53.3 0.0 copy-start
  53.4 2.5 %copy-done = f32[10,384,384]{2,1,0:T(8,128)} copy-done((f32[10,384,384]{2,1,0:T(8,128)}, f32[10,384,384]{2,1,0:T(8,128)S(1)}, u32[]{:S(2)}) %copy-start) | copy-done | bytes 5898264
  55.9 0.0 copy-start.3
  55.9 1.4 copy-done.3
  57.3 0.0 collective-permute-done.4.lower
  57.3 4.2 %collective-permute-done.5.upper = f32[1,384,384]{2,1,0:T(8,128)S(1)} collective-permute-done((f32[1,384,384]{2,1,0:T(8,128)S(1)}, f32[1,384,384]{2,1,0:T(8,128)S(1)}, u32[]{:S(2)}, u32[]{:S(2)}) %collective-permute-start.5) | collective-permute-done | bytes 589856 | tf_op jit(solution)/shard_map/ppermute | solution.py:27
  61.5 6.2 %all-gather.2.cloned.1.call-done.halo = f32[16,2,4,24,384]{4,3,2,1,0:T(8,128)} async-done(((f32[1,2,4,24,384]{4,3,2,1,0:T(8,128)}), f32[16,2,4,24,384]{4,3,2,1,0:T(8,128)}) %all-gather.2.cloned.1.call-update) | async-done | bytes 4718608 | tf_op jit(solution)/shard_map/all_gather | solution.py:410
  67.7 0.0 copy-start.1
  67.7 20.5 %vectors.1 = (f32[10,400,384]{2,1,0:T(8,128)S(1)}, f32[8,400,384]{2,1,0:T(8,128)S(1)}, f32[6,400,384]{2,1,0:T(8,128)S(1)}, f32[8,8,128]{2,1,0:T(8,128)}) custom-call(f32[4,384,384]{2,1,0:T(8,128)} %copy-done.3, f32[16,2,4,24,384]{4,3,2,1,0:T(8,128)} %all-gather.2.cloned.1.call-done.halo, f32[10,384,384]{2,1,0:T(8,128)} %copy-done), custom_call_target="tpu_custom_call" | custom-call | tf_op jit(solution)/shard_map/vectors/pallas_call | solution.py:439
  88.2 13.1 %all_to_all.10.sums = f32[8,8,128]{2,1,0:T(8,128)S(1)} all-to-all(f32[8,8,128]{2,1,0:T(8,128)} %get-tuple-element.29), channel_id=1, replica_groups=mesh['src'=32,'slab'=8] {'slab'}, dimensions={0} | all-to-all | bytes 65536 | tf_op jit(solution)/shard_map/all_to_all | solution.py:462
  101.3 0.0 copy-done.1
  101.3 6.5 %terms.1 = (f32[4,384,384]{2,1,0:T(8,128)}, f32[16,48,384]{2,1,0:T(8,128)S(1)}, f32[16,48,384]{2,1,0:T(8,128)}) custom-call(f32[8,8,128]{2,1,0:T(8,128)S(1)} %all_to_all.10.sums, f32[10,400,384]{2,1,0:T(8,128)S(1)} %get-tuple-element.30.w0, f32[8,400,384]{2,1,0:T(8,128)S(1)} %get-tuple-element.31.w1, f32[6,400,384]{2,1,0:T(8,128)S(1)} %get-tuple-element.32.w2, ...), custom_call_target="tpu_custom_call" | custom-call | tf_op jit(solution)/shard_map/terms/pallas_call | solution.py:464
  107.7 1.8 %collective-permute-start.6 = (f32[16,48,384]{2,1,0:T(8,128)}, f32[16,48,384]{2,1,0:T(8,128)S(1)}, u32[]{:S(2)}, u32[]{:S(2)}) collective-permute-start(f32[16,48,384]{2,1,0:T(8,128)} %get-tuple-element.37), channel_id=1, source_target_pairs={{0,8},{8,0},{16,24},{24,16},{32,40},{40,32},{48,56},{56,48},{64,72... | collective-permute-start | bytes 3538952 | tf_op jit(solution)/shard_map/ppermute | solution.py:478
  109.5 2.7 %collective-permute-done.6 = f32[16,48,384]{2,1,0:T(8,128)S(1)} collective-permute-done((f32[16,48,384]{2,1,0:T(8,128)}, f32[16,48,384]{2,1,0:T(8,128)S(1)}, u32[]{:S(2)}, u32[]{:S(2)}) %collective-permute-start.6) | collective-permute-done | bytes 1179680 | tf_op jit(solution)/shard_map/ppermute | solution.py:478
  112.2 0.1 add.32
  112.3 0.1 constant_dynamic-slice_fusion
  112.5 0.5 collective-permute-start.7
  112.9 1.8 %collective-permute-start.8 = (f32[4,2,24,384]{3,2,1,0:T(8,128)S(1)}, f32[4,2,24,384]{3,2,1,0:T(8,128)S(1)}, u32[]{:S(2)}, u32[]{:S(2)}) collective-permute-start(f32[4,2,24,384]{3,2,1,0:T(8,128)S(1)} %get-tuple-element.49), channel_id=1, source_target_pairs={{0,224},{8,232},{16,240},{24,248},{32,64},{40,72},{48,80},{56,88},... | collective-permute-start | bytes 884744 | tf_op jit(solution)/shard_map/ppermute | solution.py:489
  114.7 6.0 %collective-permute-done.7 = f32[4,2,24,384]{3,2,1,0:T(8,128)S(1)} collective-permute-done((f32[4,2,24,384]{3,2,1,0:T(8,128)S(1)}, f32[4,2,24,384]{3,2,1,0:T(8,128)S(1)}, u32[]{:S(2)}, u32[]{:S(2)}) %collective-permute-start.7) | collective-permute-done | bytes 294944 | tf_op jit(solution)/shard_map/ppermute | solution.py:489
  120.8 1.3 collective-permute-done.8
  122.1 0.1 maximum_add_fusion
  122.1 21.3 %all_to_all.11 = f32[8,48,384]{2,1,0:T(8,128)S(1)} all-to-all(f32[8,48,384]{2,1,0:T(8,128)S(1)} %maximum_add_fusion), channel_id=1, replica_groups={{0,16,64,80,128,144,192,208},{8,24,72,88,136,152,200,216},{32,48,96,112..., dimensions={0} | all-to-all | bytes 1179648 | tf_op jit(solution)/shard_map/all_to_all | solution.py:499
  143.5 0.7 copy.9
  (6 shorter events, 0.1 us)
Async XLA Ops:
  7.2 29.0 %copy-start.2 = (s32[4,384,384]{2,1,0:T(8,128)S(1)}, s32[4,384,384]{2,1,0:T(8,128)}, u32[]{:S(2)}) copy-start(s32[4,384,384]{2,1,0:T(8,128)} %classes.1) | copy-start | bytes 7077892
  7.2 28.9 %copy-start.6 = (f32[16]{0:T(128)S(1)}, f32[16]{0:T(128)}, u32[]{:S(2)}) copy-start(f32[16]{0:T(128)} %table.1) | copy-start | bytes 196
  7.2 60.5 %all-gather.2.cloned.1.call-start = ((), (), s32[]{:S(2)}) async-start(), calls=%async_computation.2 | async-start | bytes 5013504 | tf_op jit(solution)/shard_map/all_gather | solution.py:410
  9.3 8.6 %collective-permute-start = (f32[96,384]{1,0:T(8,128)S(1)}, f32[96,384]{1,0:T(8,128)S(1)}, u32[]{:S(2)}, u32[]{:S(2)}) collective-permute-start(f32[96,384]{1,0:T(8,128)S(1)} %bitcast.26), channel_id=1, source_target_pairs={{0,1},{1,2},{2,3},{3,4},{4,5},{5,6},{6,7},{7,0},{8,9},{9,10},{10,1... | collective-permute-start | bytes 442376 | tf_op jit(solution)/shard_map/ppermute | solution.py:27
  13.1 9.1 %collective-permute-start.1 = (f32[96,384]{1,0:T(8,128)S(1)}, f32[96,384]{1,0:T(8,128)S(1)}, u32[]{:S(2)}, u32[]{:S(2)}) collective-permute-start(f32[96,384]{1,0:T(8,128)S(1)} %bitcast.27), channel_id=1, source_target_pairs={{0,7},{1,0},{2,1},{3,2},{4,3},{5,4},{6,5},{7,6},{8,15},{9,8},{10,9... | collective-permute-start | bytes 442376 | tf_op jit(solution)/shard_map/ppermute | solution.py:27
  24.4 6.5 %copy-start.4 = (f32[9,384]{1,0:T(8,128)}, f32[9,384]{1,0:T(8,128)S(1)}, u32[]{:S(2)}) copy-start(f32[9,384]{1,0:T(8,128)S(1)} %reshape.30.own) | copy-start | bytes 41476
  24.4 6.5 %collective-permute-start.2 = (f32[9,384]{1,0:T(8,128)S(1)}, f32[9,384]{1,0:T(8,128)S(1)}, u32[]{:S(2)}, u32[]{:S(2)}) collective-permute-start(f32[9,384]{1,0:T(8,128)S(1)} %reshape.30.own), channel_id=1, source_target_pairs={{0,1},{1,2},{2,3},{3,4},{4,5},{5,6},{6,7},{7,0},{8,9},{9,10},{10,1... | collective-permute-start | bytes 41480 | tf_op jit(solution)/shard_map/ppermute | solution.py:27
  24.8 6.1 %collective-permute-start.3 = (f32[9,384]{1,0:T(8,128)S(1)}, f32[9,384]{1,0:T(8,128)S(1)}, u32[]{:S(2)}, u32[]{:S(2)}) collective-permute-start(f32[9,384]{1,0:T(8,128)S(1)} %reshape.30.own), channel_id=1, source_target_pairs={{0,7},{1,0},{2,1},{3,2},{4,3},{5,4},{6,5},{7,6},{8,15},{9,8},{10,9... | collective-permute-start | bytes 41480 | tf_op jit(solution)/shard_map/ppermute | solution.py:27
  31.0 26.3 %collective-permute-start.4 = (f32[1,384,384]{2,1,0:T(8,128)S(1)}, f32[1,384,384]{2,1,0:T(8,128)S(1)}, u32[]{:S(2)}, u32[]{:S(2)}) collective-permute-start(f32[1,384,384]{2,1,0:T(8,128)S(1)} %get-tuple-element.25), channel_id=1, source_target_pairs={{0,1},{1,2},{2,3},{3,4},{4,5},{5,6},{6,7},{7,0},{8,9},{9,10},{10,1... | collective-permute-start | bytes 1769480 | tf_op jit(solution)/shard_map/ppermute | solution.py:27
  32.6 28.8 %collective-permute-start.5 = (f32[1,384,384]{2,1,0:T(8,128)S(1)}, f32[1,384,384]{2,1,0:T(8,128)S(1)}, u32[]{:S(2)}, u32[]{:S(2)}) collective-permute-start(f32[1,384,384]{2,1,0:T(8,128)S(1)} %get-tuple-element.26), channel_id=1, source_target_pairs={{0,7},{1,0},{2,1},{3,2},{4,3},{5,4},{6,5},{7,6},{8,15},{9,8},{10,9... | collective-permute-start | bytes 1769480 | tf_op jit(solution)/shard_map/ppermute | solution.py:27
  36.1 0.7 copy-start.5
  53.3 2.5 %copy-start = (f32[10,384,384]{2,1,0:T(8,128)}, f32[10,384,384]{2,1,0:T(8,128)S(1)}, u32[]{:S(2)}) copy-start(f32[10,384,384]{2,1,0:T(8,128)S(1)} %get-tuple-element.28.right) | copy-start | bytes 17694724
  55.9 1.4 copy-start.3
  67.7 33.6 %copy-start.1 = (f32[1,4,384,384]{3,2,1,0:T(8,128)S(1)}, f32[1,4,384,384]{3,2,1,0:T(8,128)}, u32[]{:S(2)}) copy-start(f32[1,4,384,384]{3,2,1,0:T(8,128)} %param.5) | copy-start | bytes 7077892
  107.7 4.5 %collective-permute-start.6 = (f32[16,48,384]{2,1,0:T(8,128)}, f32[16,48,384]{2,1,0:T(8,128)S(1)}, u32[]{:S(2)}, u32[]{:S(2)}) collective-permute-start(f32[16,48,384]{2,1,0:T(8,128)} %get-tuple-element.37), channel_id=1, source_target_pairs={{0,8},{8,0},{16,24},{24,16},{32,40},{40,32},{48,56},{56,48},{64,72... | collective-permute-start | bytes 3538952 | tf_op jit(solution)/shard_map/ppermute | solution.py:478
  112.5 8.3 %collective-permute-start.7 = (f32[4,2,24,384]{3,2,1,0:T(8,128)S(1)}, f32[4,2,24,384]{3,2,1,0:T(8,128)S(1)}, u32[]{:S(2)}, u32[]{:S(2)}) collective-permute-start(f32[4,2,24,384]{3,2,1,0:T(8,128)S(1)} %get-tuple-element.48), channel_id=1, source_target_pairs={{0,32},{8,40},{16,48},{24,56},{32,0},{40,8},{48,16},{56,24},{64,96... | collective-permute-start | bytes 884744 | tf_op jit(solution)/shard_map/ppermute | solution.py:489
  112.9 9.1 %collective-permute-start.8 = (f32[4,2,24,384]{3,2,1,0:T(8,128)S(1)}, f32[4,2,24,384]{3,2,1,0:T(8,128)S(1)}, u32[]{:S(2)}, u32[]{:S(2)}) collective-permute-start(f32[4,2,24,384]{3,2,1,0:T(8,128)S(1)} %get-tuple-element.49), channel_id=1, source_target_pairs={{0,224},{8,232},{16,240},{24,248},{32,64},{40,72},{48,80},{56,88},... | collective-permute-start | bytes 884744 | tf_op jit(solution)/shard_map/ppermute | solution.py:489
Sparse Core Ops, SparseCore 0:
  23.1 44.5 all-gather.1
